TPU v7x, 256 devices: a whole 4x4x8 slice. The times are simulated.
256 devices in a mesh: ctx: 64 (over y_hi, z, x), head: 4 (over y_lo, core).
Axes of the slice: x: 4, y: 4 (y_hi: 2, y_lo: 2; y = y_hi * 2 + y_lo), z: 8, core: 2. Of those that a mesh axis runs over, the one named last changes fastest.
Arguments:
- qkv: bfloat16 [32768, 12288], P(('ctx', 'head')), may hold values from -26 to 26
- grad_out: bfloat16 [32768, 4096], P(('ctx', 'head')), may hold values from -6 to 6
- key_lists: int32 [256, 4], P('ctx'), may hold values from 0 to 255, as said below
- live_counts: int32 [256], P('ctx'), may hold values from 1 to 4
Outputs:
- grad_qkv: bfloat16 [32768, 12288], P(('ctx', 'head'))
Inputs may be any that keep to these rules, and one draw needn't show every extreme that they name: `key_lists`: each entry names a block whose index of ctx is within 2 of its query block's and which is not within one block of its query block; the 4 entries of a row differ. Over all 4 entries of all rows (live or not) of one index of ctx, the blocks named on any other index of ctx are at most 2 of its blocks, and this is reached.
All inputs are finite; a program needn't handle non-finite values.
Results may differ from a plain program's by a relative error of at most 0.008.
Values may be sent and summed in bfloat16 or wider, within the bound.
No kernel may reach another device: no remote copies, remote signals or barrier semaphores. Data moves between devices by JAX's collectives and lax.ppermute only.
A program may use at most 192 MiB of HBM per device.

v0:
```python
import jax
import jax.numpy as jnp
from jax import lax
from jax.sharding import PartitionSpec as P

HD = 128
BLK = 128
SEARCHER_TILES = 4
DRAWN_TARGET_SET = 4
SPAN = 2
NAMED_TILE_LIMIT = 2


def extended_2(cells, sides, width):
    for axis, dim in sides:
        count = lax.axis_size(axis)
        ends = count - 1
        head = lax.slice_in_dim(cells, 0, width, axis=dim)
        tail = lax.slice_in_dim(cells, cells.shape[dim] - width, cells.shape[dim], axis=dim)
        cells = jnp.concatenate(
            [
                lax.ppermute(tail, axis, [(i, (i + 1) % count) for i in range(ends)]),
                cells,
                lax.ppermute(head, axis, [((i + 1) % count, i) for i in range(ends)]),
            ],
            axis=dim,
        )
    return cells


def from_behind(value, axis, steps):
    count = lax.axis_size(axis)
    initial, last = (max(0, -steps), min(count, count - steps))
    return lax.ppermute(value, axis, [(source, source + steps) for source in range(initial, last)])


def block_grads(query_part, grad_part, key_part, value_part, usable):
    scaling = HD ** (-0.5)
    tile_merits = (
        jnp.einsum("qhd,nkhd->hqnk", query_part, key_part, preferred_element_type=jnp.float32)
        * scaling
    )
    weight = usable.astype(jnp.float32)[None, None, :, None]
    masked = jnp.where(weight > 0.0, tile_merits, -1e30)
    highest = jnp.max(masked, axis=(2, 3), keepdims=True)
    powers = jnp.exp(masked - highest) * weight
    soft_weights = powers / jnp.sum(powers, axis=(2, 3), keepdims=True)
    grad_soft = jnp.einsum(
        "qhd,nkhd->hqnk", grad_part, value_part, preferred_element_type=jnp.float32
    )
    row_delta = jnp.sum(soft_weights * grad_soft, axis=(2, 3), keepdims=True)
    grad_scores = soft_weights * (grad_soft - row_delta)
    soft_low = soft_weights.astype(jnp.bfloat16)
    scores_low = grad_scores.astype(jnp.bfloat16)
    grad_values = jnp.einsum(
        "hqnk,qhd->nkhd", soft_low, grad_part, preferred_element_type=jnp.float32
    )
    grad_keys = (
        jnp.einsum("hqnk,qhd->nkhd", scores_low, query_part, preferred_element_type=jnp.float32)
        * scaling
    )
    grad_query = (
        jnp.einsum("hqnk,nkhd->qhd", scores_low, key_part, preferred_element_type=jnp.float32)
        * scaling
    )
    return (grad_query, jnp.stack([grad_keys, grad_values], axis=3))


def needed_blocks(list_rows, owner_shard):
    targets = owner_shard * SEARCHER_TILES + jnp.arange(SEARCHER_TILES, dtype=jnp.int32)
    matches = list_rows[:, :, None] == targets[None, None, :]
    return jnp.any(matches, axis=(0, 1))


def slot_numbers(needed):
    block_order = jnp.arange(SEARCHER_TILES, dtype=jnp.int32)
    earlier = block_order[None, :] < block_order[:, None]
    return jnp.sum(jnp.where(earlier & needed[None, :], 1, 0), axis=1).astype(jnp.int32)


def select_table(needed):
    slot_of = slot_numbers(needed)
    slot_range = jnp.arange(NAMED_TILE_LIMIT, dtype=jnp.int32)
    return (needed[None, :] & (slot_of[None, :] == slot_range[:, None])).astype(jnp.float32)


def shards(qkv, grad_out, key_lists, live_counts):
    merged, grad_rows = (
        lax.all_to_all(qkv, "head", split_axis=1, concat_axis=0, tiled=True),
        lax.all_to_all(grad_out, "head", split_axis=1, concat_axis=0, tiled=True),
    )
    row_count = merged.shape[0]
    head_count = grad_rows.shape[1] // HD
    pair_width = head_count * 2 * HD
    per_head = merged.reshape(row_count, head_count, 3, HD)
    query_rows = per_head[:, :, 0]
    pair_rows = per_head[:, :, 1:].reshape(row_count, pair_width)
    shard_index = lax.axis_index("ctx")
    total_blocks = SEARCHER_TILES * lax.axis_size("ctx")
    local_ids = shard_index * SEARCHER_TILES + jnp.arange(SEARCHER_TILES, dtype=jnp.int32)
    window = local_ids[:, None] - 1 + jnp.arange(3, dtype=jnp.int32)[None, :]
    window_ok = (window >= 0) & (window < total_blocks)
    listed_ok = jnp.arange(DRAWN_TARGET_SET, dtype=jnp.int32)[None, :] < live_counts[:, None]
    usable = jnp.concatenate([window_ok, listed_ok], axis=1)
    offsets = [offset for offset in range(-SPAN, SPAN + 1) if offset != 0]
    owner_tables = []
    rims = extended_2(pair_rows, (("ctx", 0),), BLK)
    pieces = [rims]
    rank_list = []
    own_blocks = pair_rows.reshape(SEARCHER_TILES, BLK, pair_width)
    for offset in offsets:
        wanted = needed_blocks(key_lists, shard_index + offset)
        rank_list.append(slot_numbers(wanted))
        theirs = from_behind(key_lists, "ctx", offset)
        owner_table = select_table(needed_blocks(theirs, shard_index))
        owner_tables.append(owner_table)
        outgoing = jnp.einsum(
            "st,tbf->sbf",
            owner_table.astype(jnp.bfloat16),
            own_blocks,
            preferred_element_type=jnp.float32,
        )
        outgoing = outgoing.astype(jnp.bfloat16).reshape(NAMED_TILE_LIMIT * BLK, pair_width)
        pieces.append(from_behind(outgoing, "ctx", -offset))
    extended = jnp.concatenate(pieces, axis=0)
    rank_table = jnp.stack(rank_list)
    gap_shard = key_lists // SEARCHER_TILES - shard_index
    block_in = key_lists % SEARCHER_TILES
    side_of = jnp.where(gap_shard < 0, gap_shard + SPAN, gap_shard + SPAN - 1)
    side_hit = side_of[:, :, None] == jnp.arange(2 * SPAN, dtype=jnp.int32)[None, None, :]
    block_hit = block_in[:, :, None] == jnp.arange(SEARCHER_TILES, dtype=jnp.int32)[None, None, :]
    rank_here = jnp.sum(
        jnp.where(side_hit[:, :, :, None] & block_hit[:, :, None, :], rank_table[None, None], 0),
        axis=(2, 3),
    )
    far_place = SEARCHER_TILES + 2 + side_of * NAMED_TILE_LIMIT + rank_here
    listed_place = jnp.where(gap_shard == 0, 1 + block_in, far_place)
    window_place = jnp.clip(window - shard_index * SEARCHER_TILES + 1, 0, SEARCHER_TILES + 1)
    places = jnp.concatenate([window_place, listed_place], axis=1)
    block_count = extended.shape[0] // BLK
    tile_ordinals = extended.reshape(block_count, BLK, head_count, 2, HD)
    query_blocks = query_rows.reshape(SEARCHER_TILES, BLK, head_count, HD)
    grad_blocks = grad_rows.reshape(SEARCHER_TILES, BLK, head_count, HD)

    def step(carry, inputs):
        query_part, grad_part, block_places, block_ok = inputs
        chosen = tile_ordinals[block_places]
        grad_query, grad_pairs = block_grads(
            query_part, grad_part, chosen[:, :, :, 0], chosen[:, :, :, 1], block_ok
        )
        return (carry, (grad_query, grad_pairs))

    carry_zero = jnp.zeros((), jnp.float32)
    carry_zero, outputs = lax.scan(step, carry_zero, (query_blocks, grad_blocks, places, usable))
    grad_query, pair_terms = outputs
    slot_total = pair_terms.shape[0] * pair_terms.shape[1]
    flat_terms = pair_terms.reshape(slot_total, BLK * pair_width)
    place_flat = places.reshape(slot_total)
    owner_hits = (place_flat[None, :] == jnp.arange(block_count, dtype=jnp.int32)[:, None]).astype(
        jnp.float32
    )
    totals = jnp.dot(
        owner_hits, flat_terms, precision=lax.Precision.HIGHEST, preferred_element_type=jnp.float32
    )
    totals = totals.reshape(block_count, BLK, pair_width)
    own_grads = totals[1 : SEARCHER_TILES + 1]
    for direction in (-1, 1):
        rim_rows = totals[0] if direction == -1 else totals[SEARCHER_TILES + 1]
        arrived = from_behind(rim_rows.astype(jnp.bfloat16), "ctx", direction).astype(
            rim_rows.dtype
        )
        target_block = SEARCHER_TILES - 1 if direction == -1 else 0
        own_grads = own_grads.at[target_block].add(arrived)
    for side_index, offset in enumerate(offsets):
        first_slot = SEARCHER_TILES + 2 + side_index * NAMED_TILE_LIMIT
        arrived = from_behind(totals[first_slot : first_slot + NAMED_TILE_LIMIT], "ctx", offset)
        own_grads = own_grads + jnp.einsum(
            "st,sbf->tbf", owner_tables[side_index], arrived, precision=lax.Precision.HIGHEST
        )
    own_grads = own_grads.reshape(SEARCHER_TILES, BLK, head_count, 2, HD)
    joined = jnp.concatenate([grad_query[:, :, :, None, :], own_grads], axis=3)
    joined = joined.astype(jnp.bfloat16).reshape(row_count, head_count * 3 * HD)
    return lax.all_to_all(joined, "head", split_axis=0, concat_axis=1, tiled=True)


def solution(mesh):
    placed = (P(("ctx", "head"), None), P(("ctx", "head"), None), P("ctx", None), P("ctx"))
    return jax.shard_map(
        shards, mesh=mesh, in_specs=placed, out_specs=P(("ctx", "head"), None), check_vma=False
    )
```

profile of v0, /device:TPU:16, one launch (start us, length us, event | category | flops | bytes accessed | tf_op | source)
XLA Modules:
  0.0 709.4 jit_solution(1591707424241296608)
XLA Ops:
  7.4 8.4 %collective-permute-start.2 = (s32[4,4]{1,0:T(4,128)}, s32[4,4]{1,0:T(4,128)S(1)}, u32[]{:S(2)}, u32[]{:S(2)}) collective-permute-start(s32[4,4]{1,0:T(4,128)} %param.12), channel_id=1, source_target_pairs={{8,0},{12,4},{16,8},{20,12},{24,16},{28,20},{32,24},{36,28},{40,32... | collective-permute-start | bytes 200 | tf_op jit(solution)/shard_map/ppermute | solution.py:34
  32.4 32.0 %all-to-all-done = bf16[128,4,3072]{0,2,1:T(8,128)(2,1)S(1)} async-done(((bf16[128,4,3072]{0,2,1:T(8,128)(2,1)}), bf16[128,4,3072]{0,2,1:T(8,128)(2,1)S(1)}, u32[]{:S(2)}, u32[]{:S(2)}) %all-to-all-start) | async-done | bytes 3145760 | tf_op jit(solution)/shard_map/all_to_all | solution.py:89
  68.7 15.6 %copy.139 = bf16[4,128,3072]{1,0,2:T(4,128)(2,1)} copy(bf16[4,128,3072]{1,2,0:T(8,128)(2,1)S(1)} %bitcast.205) | data formatting | bytes 6291456 | tf_op jit(solution)/shard_map/all_to_all | solution.py:89
  102.5 8.8 %collective-permute-start.1 = (bf16[128,2048]{1,0:T(8,128)(2,1)}, bf16[128,2048]{1,0:T(8,128)(2,1)}, u32[]{:S(2)}, u32[]{:S(2)}) collective-permute-start(bf16[128,2048]{1,0:T(8,128)(2,1)} %copy.141), channel_id=1, source_target_pairs={{4,0},{8,4},{12,8},{16,12},{20,16},{24,20},{28,24},{32,28},{36,32}... | collective-permute-start | bytes 1572872 | tf_op jit(solution)/shard_map/ppermute | solution.py:24
  127.8 9.6 %collective-permute-start.7 = (bf16[256,2048]{1,0:T(8,128)(2,1)}, bf16[256,2048]{1,0:T(8,128)(2,1)}, u32[]{:S(2)}, u32[]{:S(2)}) collective-permute-start(bf16[256,2048]{1,0:T(8,128)(2,1)} %bitcast.38), channel_id=1, source_target_pairs={{4,0},{8,4},{12,8},{16,12},{20,16},{24,20},{28,24},{32,28},{36,32}... | collective-permute-start | bytes 3145736 | tf_op jit(solution)/shard_map/ppermute | solution.py:34
  160.5 18.6 %collective-permute-done.5 = bf16[256,2048]{1,0:T(8,128)(2,1)} collective-permute-done((bf16[256,2048]{1,0:T(8,128)(2,1)}, bf16[256,2048]{1,0:T(8,128)(2,1)}, u32[]{:S(2)}, u32[]{:S(2)}) %collective-permute-start.5) | collective-permute-done | bytes 1048608 | tf_op jit(solution)/shard_map/ppermute | solution.py:34
  181.5 27.0 %collective-permute-done.7 = bf16[256,2048]{1,0:T(8,128)(2,1)} collective-permute-done((bf16[256,2048]{1,0:T(8,128)(2,1)}, bf16[256,2048]{1,0:T(8,128)(2,1)}, u32[]{:S(2)}, u32[]{:S(2)}) %collective-permute-start.7) | collective-permute-done | bytes 1048608 | tf_op jit(solution)/shard_map/ppermute | solution.py:34
  211.9 12.6 %reshape.229 = bf16[14,128,8,2,128]{4,3,2,1,0:T(2,128)(2,1)} reshape(bf16[1792,2048]{1,0:T(8,128)(2,1)} %constant_dynamic-update-slice_fusion) | data formatting | bytes 14680064 | tf_op jit(solution)/shard_map/reshape | solution.py:141
  224.5 7.5 %copy.154 = bf16[14,128,8,2,128]{4,2,3,1,0:T(8,128)(2,1)} copy(bf16[14,128,8,2,128]{4,3,2,1,0:T(2,128)(2,1)} %reshape.229) | data formatting | bytes 14680064 | tf_op jit(solution)/shard_map/while | solution.py:154
  232.0 143.2 %while.14 = (s32[]{:T(128)}, bf16[4,128,8,128]{1,3,2,0:T(8,128)(2,1)S(1)}, f32[4,7,128,8,2,128]{5,4,3,2,1,0:T(2,128)}, s32[4,7]{1,0:T(4,128)S(1)}, bf16[14,128,8...) while((s32[]{:T(128)}, ...), condition=%wide.region_21.22_spmd, body=%wide.region_17.21_spmd.sunk | while | flops 1203894272 | bytes 104907184 | solution.py:154
  232.4 6.1 gather_fusion
  256.4 11.7 %copy_dynamic-update-slice_fusion.2 = f32[4,7,128,8,2,128]{5,4,3,2,1,0:T(2,128)} fusion(f32[4,7,128,8,2,128]{5,4,3,2,1,0:T(2,128)} %get-tuple-element.224, s32[]{:T(128)S(6)} %copy.226, f32[1,7,128,8,2,128]{5,2,1,3,4,0:T(8,128)} %maximum_bitcast_fusion.2), kind=kLoop, calls=%fused_computation.2.clone.1 | loop fusion | bytes 14680068 | tf_op jit(solution)/shard_map/while/body/jit(dynamic_update_index_in_dim)/dynamic_update_slice | solution.py:154
  268.0 6.1 gather_fusion
  292.0 11.8 %copy_dynamic-update-slice_fusion.2 = f32[4,7,128,8,2,128]{5,4,3,2,1,0:T(2,128)} fusion(f32[4,7,128,8,2,128]{5,4,3,2,1,0:T(2,128)} %get-tuple-element.224, s32[]{:T(128)S(6)} %copy.226, f32[1,7,128,8,2,128]{5,2,1,3,4,0:T(8,128)} %maximum_bitcast_fusion.2), kind=kLoop, calls=%fused_computation.2.clone.1 | loop fusion | bytes 14680068 | tf_op jit(solution)/shard_map/while/body/jit(dynamic_update_index_in_dim)/dynamic_update_slice | solution.py:154
  303.8 6.1 gather_fusion
  327.7 11.8 %copy_dynamic-update-slice_fusion.2 = f32[4,7,128,8,2,128]{5,4,3,2,1,0:T(2,128)} fusion(f32[4,7,128,8,2,128]{5,4,3,2,1,0:T(2,128)} %get-tuple-element.224, s32[]{:T(128)S(6)} %copy.226, f32[1,7,128,8,2,128]{5,2,1,3,4,0:T(8,128)} %maximum_bitcast_fusion.2), kind=kLoop, calls=%fused_computation.2.clone.1 | loop fusion | bytes 14680068 | tf_op jit(solution)/shard_map/while/body/jit(dynamic_update_index_in_dim)/dynamic_update_slice | solution.py:154
  363.4 11.7 %copy_dynamic-update-slice_fusion.2 = f32[4,7,128,8,2,128]{5,4,3,2,1,0:T(2,128)} fusion(f32[4,7,128,8,2,128]{5,4,3,2,1,0:T(2,128)} %get-tuple-element.224, s32[]{:T(128)S(6)} %copy.226, f32[1,7,128,8,2,128]{5,2,1,3,4,0:T(8,128)} %maximum_bitcast_fusion.2), kind=kLoop, calls=%fused_computation.2.clone.1 | loop fusion | bytes 14680068 | tf_op jit(solution)/shard_map/while/body/jit(dynamic_update_index_in_dim)/dynamic_update_slice | solution.py:154
  375.2 51.0 %reshape.231 = f32[28,262144]{1,0:T(8,128)} reshape(f32[4,7,128,8,2,128]{5,4,3,2,1,0:T(2,128)} %get-tuple-element.73) | data formatting | bytes 58720256 | tf_op jit(solution)/shard_map/reshape | solution.py:157
  426.2 25.8 %fusion.84 = (bf16[14,262144]{1,0:T(8,128)(2,1)}, f32[14,262144]{1,0:T(8,128)}) fusion(f32[28,262144]{1,0:T(8,128)} %reshape.231, s32[28]{0:T(128)S(1)} %copy-done.27), kind=kOutput, calls=%fused_computation.152 | convolution fusion | flops 1236795776 | bytes 51380336 | tf_op jit(solution)/shard_map/dot_general | solution.py:162
  452.0 15.1 %fusion.82 = (f32[2,262144]{1,0:T(2,128)}, f32[2,262144]{1,0:T(2,128)}, f32[2,262144]{1,0:T(2,128)}, f32[2,262144]{1,0:T(2,128)}) fusion(f32[14,262144]{1,0:T(8,128)} %get-tuple-element.145), kind=kLoop, calls=%fused_computation.150 | loop fusion | bytes 16777216 | tf_op jit(solution)/shard_map/slice | solution.py:176
  469.0 9.6 %collective-permute-start.13 = (f32[2,128,2048]{2,0,1:T(2,128)}, f32[2,128,2048]{2,0,1:T(2,128)}, u32[]{:S(2)}, u32[]{:S(2)}) collective-permute-start(f32[2,128,2048]{2,0,1:T(2,128)} %bitcast.50), channel_id=1, source_target_pairs={{4,0},{8,4},{12,8},{16,12},{20,16},{24,20},{28,24},{32,28},{36,32}... | collective-permute-start | bytes 6291464 | tf_op jit(solution)/shard_map/ppermute | solution.py:34
  478.7 13.9 %slice_reduce_fusion = (bf16[262144]{0:T(1024)(128)(2,1)S(1)}, bf16[262144]{0:T(1024)(128)(2,1)S(1)}) fusion(bf16[14,262144]{1,0:T(8,128)(2,1)} %get-tuple-element.144), kind=kLoop, calls=%fused_computation.47 | loop fusion | bytes 2097152 | tf_op jit(solution)/shard_map/slice | solution.py:168
  501.6 13.2 %slice_reduce_fusion.2 = f32[262144]{0:T(1024)S(1)} fusion(f32[14,262144]{1,0:T(8,128)} %get-tuple-element.145), kind=kLoop, calls=%fused_computation.50 | loop fusion | bytes 2097152 | tf_op jit(solution)/shard_map/slice.64
  520.2 45.1 %collective-permute-done.10 = bf16[128,2048]{1,0:T(8,128)(2,1)S(1)} collective-permute-done((bf16[128,2048]{1,0:T(8,128)(2,1)S(1)}, bf16[128,2048]{1,0:T(8,128)(2,1)S(1)}, u32[]{:S(2)}, u32[]{:S(2)}) %collective-permute-start.10) | collective-permute-done | bytes 524320 | tf_op jit(solution)/shard_map/ppermute | solution.py:34
  569.9 19.9 %scatter-add.6 = f32[4,128,2048]{2,0,1:T(4,128)} dynamic-update-slice(f32[4,128,2048]{2,0,1:T(4,128)} %bitcast.203, f32[1,128,2048]{2,0,1:T(1,128)S(1)} %add.185, s32[]{:T(128)} %constant.137.clone.1, s32[]{:T(128)} %constant.129.clone.1, s32[]{:T(128)} %constant.129.clone.1) | dynamic-update-slice | bytes 2097156 | tf_op jit(solution)/shard_map/scatter-add | solution.py:173
  593.8 19.5 %scatter-add.9 = f32[4,128,2048]{2,0,1:T(4,128)} dynamic-update-slice(f32[4,128,2048]{2,0,1:T(4,128)} %scatter-add.6, f32[1,128,2048]{2,0,1:T(1,128)S(1)} %slice_add_fusion, s32[]{:T(128)} %constant.129.clone.1, s32[]{:T(128)} %constant.129.clone.1, s32[]{:T(128)} %constant.129.clone.1) | dynamic-update-slice | bytes 2097156 | tf_op jit(solution)/shard_map/scatter-add | solution.py:173
  613.3 6.4 fusion.54
  619.8 6.4 fusion.56
  626.2 6.5 fusion.58
  632.8 21.7 %collective-permute-done.15 = f32[2,128,2048]{2,0,1:T(2,128)S(1)} collective-permute-done((f32[2,128,2048]{2,0,1:T(2,128)}, f32[2,128,2048]{2,0,1:T(2,128)S(1)}, u32[]{:S(2)}, u32[]{:S(2)}) %collective-permute-start.15) | collective-permute-done | bytes 2097184 | tf_op jit(solution)/shard_map/ppermute | solution.py:34
  654.4 8.7 %add_convert_fusion = bf16[4,128,2048]{2,0,1:T(4,128)(2,1)} fusion(f32[4,128,2048]{2,0,1:T(4,128)S(1)} %fusion.54, f32[4,128,2048]{2,0,1:T(4,128)S(1)} %fusion.56, f32[4,128,2048]{2,0,1:T(4,128)S(1)} %copy-done, f32[4,128,2048]{2,0,1:T(4,128)S(1)} %fusion.58, f32[2,128,2048]{2,0,1:T(2,128)S(1)} %collective-permute-done.15, pred[4]{0:T(512)(128)(4,1)S(1)} %copy-done.12, ...), kind=kOutput, calls=%fused_computation.41 | convolution fusion | flops 30408720 | bytes 20971540 | tf_op jit(solution)/shard_map/st,sbf->tbf/dot_general | solution.py:177
  667.0 39.4 %all_to_all.48 = bf16[4,128,3072]{1,2,0:T(8,128)(2,1)S(1)} all-to-all(bf16[4,128,3072]{1,2,0:T(8,128)(2,1)S(1)} %bitcast.207), channel_id=1, replica_groups=mesh['ctx'=64,'head'=4] {'head'}, dimensions={0} | all-to-all | bytes 6291456 | tf_op jit(solution)/shard_map/all_to_all | solution.py:183
  (218 shorter events, 200.1 us)
Async XLA Ops:
  0.0 31.9 %collective-permute-start.8 = (s32[4,4]{1,0:T(4,128)}, s32[4,4]{1,0:T(4,128)S(1)}, u32[]{:S(2)}, u32[]{:S(2)}) collective-permute-start(s32[4,4]{1,0:T(4,128)} %param.12), channel_id=1, source_target_pairs={{0,8},{4,12},{8,16},{12,20},{16,24},{20,28},{24,32},{28,36},{32,40... | collective-permute-start | bytes 200 | tf_op jit(solution)/shard_map/ppermute | solution.py:34
  4.9 26.9 %collective-permute-start.6 = (s32[4,4]{1,0:T(4,128)}, s32[4,4]{1,0:T(4,128)S(1)}, u32[]{:S(2)}, u32[]{:S(2)}) collective-permute-start(s32[4,4]{1,0:T(4,128)} %param.12), channel_id=1, source_target_pairs={{0,4},{4,8},{8,12},{12,16},{16,20},{20,24},{24,28},{28,32},{32,36}... | collective-permute-start | bytes 200 | tf_op jit(solution)/shard_map/ppermute | solution.py:34
  7.4 24.4 %collective-permute-start.2 = (s32[4,4]{1,0:T(4,128)}, s32[4,4]{1,0:T(4,128)S(1)}, u32[]{:S(2)}, u32[]{:S(2)}) collective-permute-start(s32[4,4]{1,0:T(4,128)} %param.12), channel_id=1, source_target_pairs={{8,0},{12,4},{16,8},{20,12},{24,16},{28,20},{32,24},{36,28},{40,32... | collective-permute-start | bytes 200 | tf_op jit(solution)/shard_map/ppermute | solution.py:34
  15.9 16.0 %collective-permute-start.4 = (s32[4,4]{1,0:T(4,128)}, s32[4,4]{1,0:T(4,128)S(1)}, u32[]{:S(2)}, u32[]{:S(2)}) collective-permute-start(s32[4,4]{1,0:T(4,128)} %param.12), channel_id=1, source_target_pairs={{4,0},{8,4},{12,8},{16,12},{20,16},{24,20},{28,24},{32,28},{36,32}... | collective-permute-start | bytes 200 | tf_op jit(solution)/shard_map/ppermute | solution.py:34
  23.7 40.7 %all-to-all-start = ((bf16[128,4,3072]{0,2,1:T(8,128)(2,1)}), bf16[128,4,3072]{0,2,1:T(8,128)(2,1)S(1)}, u32[]{:S(2)}, u32[]{:S(2)}) async-start(bf16[128,4,3072]{0,2,1:T(8,128)(2,1)} %bitcast.206), calls=%async_computation | async-start | bytes 6291456 | tf_op jit(solution)/shard_map/all_to_all | solution.py:89
  32.0 84.0 %copy-start.13 = (pred[4]{0:T(512)(128)(4,1)}, pred[4]{0:T(512)(128)(4,1)S(1)}, u32[]{:S(2)}) copy-start(pred[4]{0:T(512)(128)(4,1)S(1)} %get-tuple-element.114) | copy-start | bytes 16
  32.0 88.7 %copy-start.15 = (pred[4]{0:T(512)(128)(4,1)}, pred[4]{0:T(512)(128)(4,1)S(1)}, u32[]{:S(2)}) copy-start(pred[4]{0:T(512)(128)(4,1)S(1)} %get-tuple-element.115) | copy-start | bytes 16
  32.0 93.2 %copy-start.17 = (pred[4]{0:T(512)(128)(4,1)}, pred[4]{0:T(512)(128)(4,1)S(1)}, u32[]{:S(2)}) copy-start(pred[4]{0:T(512)(128)(4,1)S(1)} %get-tuple-element.113) | copy-start | bytes 16
  32.0 105.5 %copy-start.11 = (pred[4]{0:T(512)(128)(4,1)}, pred[4]{0:T(512)(128)(4,1)S(1)}, u32[]{:S(2)}) copy-start(pred[4]{0:T(512)(128)(4,1)S(1)} %get-tuple-element.112) | copy-start | bytes 16
  32.2 83.8 %copy-start.21 = (s32[4]{0:T(128)}, s32[4]{0:T(128)S(1)}, u32[]{:S(2)}) copy-start(s32[4]{0:T(128)S(1)} %get-tuple-element.155) | copy-start | bytes 52
  32.2 88.5 %copy-start.23 = (s32[4]{0:T(128)}, s32[4]{0:T(128)S(1)}, u32[]{:S(2)}) copy-start(s32[4]{0:T(128)S(1)} %get-tuple-element.154) | copy-start | bytes 52
  32.4 92.9 %copy-start.25 = (s32[4]{0:T(128)}, s32[4]{0:T(128)S(1)}, u32[]{:S(2)}) copy-start(s32[4]{0:T(128)S(1)} %get-tuple-element.153) | copy-start | bytes 52
  32.4 105.1 %copy-start.19 = (s32[4]{0:T(128)}, s32[4]{0:T(128)S(1)}, u32[]{:S(2)}) copy-start(s32[4]{0:T(128)S(1)} %get-tuple-element.152) | copy-start | bytes 52
  64.4 167.6 %all-to-all-start.1 = ((bf16[128,4,1024]{0,2,1:T(8,128)(2,1)}), bf16[128,4,1024]{0,2,1:T(8,128)(2,1)}, u32[]{:S(2)}, u32[]{:S(2)}) async-start(bf16[128,4,1024]{0,2,1:T(8,128)(2,1)} %bitcast.211), calls=%async_computation.1 | async-start | bytes 2097152 | tf_op jit(solution)/shard_map/all_to_all | solution.py:90
  94.1 49.2 %collective-permute-start = (bf16[128,2048]{1,0:T(8,128)(2,1)}, bf16[128,2048]{1,0:T(8,128)(2,1)}, u32[]{:S(2)}, u32[]{:S(2)}) collective-permute-start(bf16[128,2048]{1,0:T(8,128)(2,1)} %copy.140), channel_id=1, source_target_pairs={{0,4},{4,8},{8,12},{12,16},{16,20},{20,24},{24,28},{28,32},{32,36}... | collective-permute-start | bytes 1572872 | tf_op jit(solution)/shard_map/ppermute | solution.py:22
  102.5 48.4 %collective-permute-start.1 = (bf16[128,2048]{1,0:T(8,128)(2,1)}, bf16[128,2048]{1,0:T(8,128)(2,1)}, u32[]{:S(2)}, u32[]{:S(2)}) collective-permute-start(bf16[128,2048]{1,0:T(8,128)(2,1)} %copy.141), channel_id=1, source_target_pairs={{4,0},{8,4},{12,8},{16,12},{20,16},{24,20},{28,24},{32,28},{36,32}... | collective-permute-start | bytes 1572872 | tf_op jit(solution)/shard_map/ppermute | solution.py:24
  118.6 39.6 %collective-permute-start.3 = (bf16[256,2048]{1,0:T(8,128)(2,1)}, bf16[256,2048]{1,0:T(8,128)(2,1)}, u32[]{:S(2)}, u32[]{:S(2)}) collective-permute-start(bf16[256,2048]{1,0:T(8,128)(2,1)} %bitcast.34), channel_id=1, source_target_pairs={{0,8},{4,12},{8,16},{12,20},{16,24},{20,28},{24,32},{28,36},{32,40... | collective-permute-start | bytes 3145736 | tf_op jit(solution)/shard_map/ppermute | solution.py:34
  123.3 55.8 %collective-permute-start.5 = (bf16[256,2048]{1,0:T(8,128)(2,1)}, bf16[256,2048]{1,0:T(8,128)(2,1)}, u32[]{:S(2)}, u32[]{:S(2)}) collective-permute-start(bf16[256,2048]{1,0:T(8,128)(2,1)} %bitcast.36), channel_id=1, source_target_pairs={{0,4},{4,8},{8,12},{12,16},{16,20},{20,24},{24,28},{28,32},{32,36}... | collective-permute-start | bytes 3145736 | tf_op jit(solution)/shard_map/ppermute | solution.py:34
  127.8 80.7 %collective-permute-start.7 = (bf16[256,2048]{1,0:T(8,128)(2,1)}, bf16[256,2048]{1,0:T(8,128)(2,1)}, u32[]{:S(2)}, u32[]{:S(2)}) collective-permute-start(bf16[256,2048]{1,0:T(8,128)(2,1)} %bitcast.38), channel_id=1, source_target_pairs={{4,0},{8,4},{12,8},{16,12},{20,16},{24,20},{28,24},{32,28},{36,32}... | collective-permute-start | bytes 3145736 | tf_op jit(solution)/shard_map/ppermute | solution.py:34
  143.3 67.6 %collective-permute-start.9 = (bf16[256,2048]{1,0:T(8,128)(2,1)}, bf16[256,2048]{1,0:T(8,128)(2,1)S(1)}, u32[]{:S(2)}, u32[]{:S(2)}) collective-permute-start(bf16[256,2048]{1,0:T(8,128)(2,1)} %bitcast.215), channel_id=1, source_target_pairs={{8,0},{12,4},{16,8},{20,12},{24,16},{28,20},{32,24},{36,28},{40,32... | collective-permute-start | bytes 3145736 | tf_op jit(solution)/shard_map/ppermute | solution.py:34
  375.2 51.0 %copy-start.7 = (bf16[4,128,8,128]{1,3,2,0:T(8,128)(2,1)}, bf16[4,128,8,128]{1,3,2,0:T(8,128)(2,1)S(1)}, u32[]{:S(2)}) copy-start(bf16[4,128,8,128]{1,3,2,0:T(8,128)(2,1)S(1)} %get-tuple-element.72) | copy-start | bytes 3145732
  375.2 51.0 %copy-start.27 = (s32[28]{0:T(128)S(1)}, s32[28]{0:T(128)}, u32[]{:S(2)}) copy-start(s32[28]{0:T(128)} %eq.235) | copy-start | bytes 340
  467.1 146.2 %collective-permute-start.14 = (f32[2,128,2048]{2,0,1:T(2,128)}, f32[2,128,2048]{2,0,1:T(2,128)}, u32[]{:S(2)}, u32[]{:S(2)}) collective-permute-start(f32[2,128,2048]{2,0,1:T(2,128)} %bitcast.52), channel_id=1, source_target_pairs={{0,4},{4,8},{8,12},{12,16},{16,20},{20,24},{24,28},{28,32},{32,36}... | collective-permute-start | bytes 6291464 | tf_op jit(solution)/shard_map/ppermute | solution.py:34
  469.0 150.7 %collective-permute-start.13 = (f32[2,128,2048]{2,0,1:T(2,128)}, f32[2,128,2048]{2,0,1:T(2,128)}, u32[]{:S(2)}, u32[]{:S(2)}) collective-permute-start(f32[2,128,2048]{2,0,1:T(2,128)} %bitcast.50), channel_id=1, source_target_pairs={{4,0},{8,4},{12,8},{16,12},{20,16},{24,20},{28,24},{32,28},{36,32}... | collective-permute-start | bytes 6291464 | tf_op jit(solution)/shard_map/ppermute | solution.py:34
  492.8 72.5 %collective-permute-start.10 = (bf16[128,2048]{1,0:T(8,128)(2,1)S(1)}, bf16[128,2048]{1,0:T(8,128)(2,1)S(1)}, u32[]{:S(2)}, u32[]{:S(2)}) collective-permute-start(bf16[128,2048]{1,0:T(8,128)(2,1)S(1)} %convert_element_type.86), channel_id=1, source_target_pairs={{4,0},{8,4},{12,8},{16,12},{20,16},{24,20},{28,24},{32,28},{36,32}... | collective-permute-start | bytes 1572872 | tf_op jit(solution)/shard_map/ppermute | solution.py:34
  495.8 94.0 %collective-permute-start.11 = (bf16[128,2048]{1,0:T(8,128)(2,1)}, bf16[128,2048]{1,0:T(8,128)(2,1)}, u32[]{:S(2)}, u32[]{:S(2)}) collective-permute-start(bf16[128,2048]{1,0:T(8,128)(2,1)} %convert_element_type.88), channel_id=1, source_target_pairs={{0,4},{4,8},{8,12},{12,16},{16,20},{20,24},{24,28},{28,32},{32,36}... | collective-permute-start | bytes 1572872 | tf_op jit(solution)/shard_map/ppermute | solution.py:34
  499.7 126.5 %collective-permute-start.12 = (f32[2,128,2048]{2,0,1:T(2,128)}, f32[2,128,2048]{2,0,1:T(2,128)}, u32[]{:S(2)}, u32[]{:S(2)}) collective-permute-start(f32[2,128,2048]{2,0,1:T(2,128)} %bitcast.48), channel_id=1, source_target_pairs={{8,0},{12,4},{16,8},{20,12},{24,16},{28,20},{32,24},{36,28},{40,32... | collective-permute-start | bytes 6291464 | tf_op jit(solution)/shard_map/ppermute | solution.py:34
  566.1 88.3 %collective-permute-start.15 = (f32[2,128,2048]{2,0,1:T(2,128)}, f32[2,128,2048]{2,0,1:T(2,128)S(1)}, u32[]{:S(2)}, u32[]{:S(2)}) collective-permute-start(f32[2,128,2048]{2,0,1:T(2,128)} %bitcast.214), channel_id=1, source_target_pairs={{0,8},{4,12},{8,16},{12,20},{16,24},{20,28},{24,32},{28,36},{32,40... | collective-permute-start | bytes 6291464 | tf_op jit(solution)/shard_map/ppermute | solution.py:34
  589.8 23.5 %copy-start.26 = (s32[4]{0:T(128)S(1)}, s32[4]{0:T(128)}, u32[]{:S(2)}) copy-start(s32[4]{0:T(128)} %copy-done.25) | copy-start | bytes 52
  626.2 28.3 %copy-start = (f32[4,128,2048]{2,0,1:T(4,128)S(1)}, f32[4,128,2048]{2,0,1:T(4,128)}, u32[]{:S(2)}) copy-start(f32[4,128,2048]{2,0,1:T(4,128)} %scatter-add.9) | copy-start | bytes 12582916
  626.2 28.3 %copy-start.12 = (pred[4]{0:T(512)(128)(4,1)S(1)}, pred[4]{0:T(512)(128)(4,1)}, u32[]{:S(2)}) copy-start(pred[4]{0:T(512)(128)(4,1)} %copy-done.11) | copy-start | bytes 16
  626.2 28.3 %copy-start.20 = (s32[4]{0:T(128)S(1)}, s32[4]{0:T(128)}, u32[]{:S(2)}) copy-start(s32[4]{0:T(128)} %copy-done.19) | copy-start | bytes 52
  (16 other events, 119.0 us)
where the time goes:
time: 723 us; the launch traced here: 709 us
  local copies, waits for them, and re-layouts  318 us (44%)
  waiting for transfers between devices  150 us (21%)
  matrix products  83.8 us (12%)
  starting transfers between devices  77.8 us (11%)
  blocking collectives  39.4 us (5%)
  other arithmetic  38.5 us (5%)
    ppermute x14, waiting for transfers between devices, from_behind(): lax.ppermute(value, axis, [(source, source + steps) for source in range(i...  118 us
    ppermute x14, starting transfers between devices, from_behind(): lax.ppermute(value, axis, [(source, source + steps) for source in range(i...  58.1 us
    reshape x1, local copies, waits for them, and re-layouts, shards(): flat_terms = pair_terms.reshape(slot_total, BLK * pair_width)  51 us
    dynamic_update_slice x4, local copies, waits for them, and re-layouts, shards(): lax.scan(step, carry_zero, (query_blocks, grad_blocks, places, usable))  46.9 us
    all_to_all x1, blocking collectives, shards(): lax.all_to_all(joined, 'head', split_axis=0, concat_axis=1, tiled=True)  39.4 us
    scatter-add x2, local copies, waits for them, and re-layouts, shards(): own_grads = own_grads.at[target_block].add(arrived)  39.4 us
    all_to_all x1, waiting for transfers between devices, shards(): lax.all_to_all(qkv, 'head', split_axis=1, concat_axis=0, tiled=True)  32 us
    dot_general x4, matrix products, shards(): jnp.einsum('st,sbf->tbf', owner_tables[side_index], arrived, precision=la...  28 us
  transfers between devices with their start and end apart: 18, of which 6 were waited for; matrix products, arithmetic and copies ran while one was open for 27% of the time, Pallas kernels for 0%

commit v1 on v0

v1 whole, which is shorter than its diff:
```python
import functools

import jax
import jax.numpy as jnp
from jax import lax
from jax.experimental import pallas as pl
from jax.experimental.pallas import tpu as pltpu
from jax.sharding import Mesh
from jax.sharding import PartitionSpec as P

HD = 128
BLK = 128
TILES = 4
SPAN = 2
LISTED = 4
WIN = 3
RING = 4
GROUP = RING * TILES
HALO = SPAN * TILES
EXT = GROUP + 2 * HALO
LOCAL = 2
SLOTS = WIN + LISTED
COLS = LOCAL * 3 * HD
LOG2E = 1.4426950408889634
F32 = jnp.float32
BF16 = jnp.bfloat16


PAIR = 2


def send_kernel(flip_ref, qkv_ref, grad_ref, kv_ref, qd_ref):
    for part in range(PAIR):
        for h in range(LOCAL):
            at = (part * LOCAL + h) * 3 * HD
            gat = (part * LOCAL + h) * HD
            kv_ref[part, h] = qkv_ref[:, at + HD : at + 3 * HD]
            qd_ref[part, h, :, 0:HD] = qkv_ref[:, at : at + HD]
            qd_ref[part, h, :, HD : 2 * HD] = grad_ref[:, gat : gat + HD]


def split_heads(flip, qkv, grad_out):
    def there(g, flip_ref):
        return (jnp.bitwise_xor(g, flip_ref[0]), 0, 0, 0)

    parts = jax.ShapeDtypeStruct((GROUP, LOCAL, BLK, 2 * HD), BF16)
    return pl.pallas_call(
        send_kernel,
        out_shape=[parts, parts],
        grid_spec=pltpu.PrefetchScalarGridSpec(
            num_scalar_prefetch=1,
            grid=(GROUP // PAIR,),
            in_specs=[
                pl.BlockSpec((BLK, PAIR * COLS), lambda g, f: (0, g)),
                pl.BlockSpec((BLK, PAIR * LOCAL * HD), lambda g, f: (0, g)),
            ],
            out_specs=[
                pl.BlockSpec((PAIR, LOCAL, BLK, 2 * HD), there),
                pl.BlockSpec((PAIR, LOCAL, BLK, 2 * HD), there),
            ],
        ),
        cost_estimate=pl.CostEstimate(flops=0, bytes_accessed=8 << 20, transcendentals=0),
    )(flip, qkv, grad_out)


def join_kernel(flip_ref, dq_ref, dkv_ref, out_ref):
    for part in range(PAIR):
        for h in range(LOCAL):
            at = (part * LOCAL + h) * 3 * HD
            out_ref[:, at : at + HD] = dq_ref[part, h]
            out_ref[:, at + HD : at + 3 * HD] = dkv_ref[part, h]


def join_heads(flip, dq, dkv):
    def there(g, flip_ref):
        return (jnp.bitwise_xor(g, flip_ref[0]), 0, 0, 0)

    return pl.pallas_call(
        join_kernel,
        out_shape=jax.ShapeDtypeStruct((BLK, GROUP * COLS), BF16),
        grid_spec=pltpu.PrefetchScalarGridSpec(
            num_scalar_prefetch=1,
            grid=(GROUP // PAIR,),
            in_specs=[
                pl.BlockSpec((PAIR, LOCAL, BLK, HD), there),
                pl.BlockSpec((PAIR, LOCAL, BLK, 2 * HD), there),
            ],
            out_specs=pl.BlockSpec((BLK, PAIR * COLS), lambda g, f: (0, g)),
        ),
        cost_estimate=pl.CostEstimate(flops=0, bytes_accessed=6 << 20, transcendentals=0),
    )(flip, dq, dkv)


def attention_kernel(
    head,
    place_ref,
    live_ref,
    kv_ref,
    before_ref,
    after_ref,
    qd_ref,
    dq_ref,
    own_ref,
    tobefore_ref,
    toafter_ref,
    kv,
    qd,
    acc,
    mix,
    tall,
    low,
    dqs,
    outs,
    sem,
):
    loads = [
        pltpu.make_async_copy(before_ref.at[:, head], kv.at[pl.ds(0, HALO)], sem.at[0]),
        pltpu.make_async_copy(kv_ref.at[:, head], kv.at[pl.ds(HALO, GROUP)], sem.at[1]),
        pltpu.make_async_copy(after_ref.at[:, head], kv.at[pl.ds(HALO + GROUP, HALO)], sem.at[2]),
        pltpu.make_async_copy(qd_ref.at[:, head], qd, sem.at[3]),
    ]
    for c in loads:
        c.start()
    acc[...] = jnp.zeros_like(acc)
    mix[...] = jnp.zeros_like(mix)
    for c in loads:
        c.wait()
    scale = HD ** (-0.5)

    def one_block(block, _):
        mix[0:BLK, 0:HD] = qd[block, :, 0:HD]
        mix[BLK : 2 * BLK, HD : 2 * HD] = qd[block, :, HD : 2 * HD]
        weights = mix[...]
        high = jnp.full((8, BLK), -3e38, F32)
        for j in range(SLOTS):
            place = place_ref[block, j]
            both = lax.dot_general(
                kv[place], weights, (((1,), (1,)), ((), ())), preferred_element_type=F32
            )
            bias = jnp.where(live_ref[block, j] > 0, 0.0, -1e30).astype(F32)
            scores = both[:, 0:BLK] * (scale * LOG2E) + bias
            tall[j, :, 0:BLK] = scores
            tall[j, :, BLK : 2 * BLK] = both[:, BLK : 2 * BLK]
            high = jnp.maximum(high, jnp.max(scores.reshape(BLK // 8, 8, BLK), axis=0))
        top = jnp.max(high, axis=0, keepdims=True)
        total = jnp.zeros((8, BLK), F32)
        cross = jnp.zeros((8, BLK), F32)
        for j in range(SLOTS):
            powers = jnp.exp2(tall[j, :, 0:BLK] - top)
            tall[j, :, 0:BLK] = powers
            total = total + jnp.sum(powers.reshape(BLK // 8, 8, BLK), axis=0)
            cross = cross + jnp.sum(
                (powers * tall[j, :, BLK : 2 * BLK]).reshape(BLK // 8, 8, BLK), axis=0
            )
        inverse = 1.0 / jnp.sum(total, axis=0, keepdims=True)
        delta = jnp.sum(cross, axis=0, keepdims=True) * inverse
        grad_query = jnp.zeros((BLK, HD), F32)
        for j in range(SLOTS):
            place = place_ref[block, j]
            soft = tall[j, :, 0:BLK] * inverse
            grads = (soft * (tall[j, :, BLK : 2 * BLK] - delta)).astype(BF16)
            low[j, :, 0:BLK] = grads
            low[j, :, BLK : 2 * BLK] = soft.astype(BF16)
            grad_query = grad_query + lax.dot_general(
                grads, kv[place, :, 0:HD], (((0,), (0,)), ((), ())), preferred_element_type=F32
            )
            acc[place] += lax.dot_general(
                low[j], weights, (((1,), (0,)), ((), ())), preferred_element_type=F32
            )
        dqs[block] = (grad_query * scale).astype(BF16)
        return 0

    lax.fori_loop(0, GROUP, one_block, 0)

    def finish(place, _):
        acc[place, :, 0:HD] = acc[place, :, 0:HD] * scale
        return 0

    lax.fori_loop(0, EXT, finish, 0)
    outs[0:HALO] = acc[0:HALO].astype(BF16)
    outs[HALO : 2 * HALO] = acc[HALO + GROUP : EXT].astype(BF16)
    stores = [
        pltpu.make_async_copy(dqs, dq_ref, sem.at[0]),
        pltpu.make_async_copy(acc.at[pl.ds(HALO, GROUP)], own_ref, sem.at[1]),
        pltpu.make_async_copy(outs.at[pl.ds(0, HALO)], tobefore_ref, sem.at[2]),
        pltpu.make_async_copy(outs.at[pl.ds(HALO, HALO)], toafter_ref, sem.at[3]),
    ]
    for c in stores:
        c.start()
    for c in stores:
        c.wait()


def attention(head, places, live, kv, before, after, qd):
    hbm = pl.BlockSpec(memory_space=pl.ANY)
    smem = pl.BlockSpec(memory_space=pltpu.SMEM)
    return pl.pallas_call(
        functools.partial(attention_kernel, head),
        out_shape=[
            jax.ShapeDtypeStruct((GROUP, BLK, HD), BF16),
            jax.ShapeDtypeStruct((GROUP, BLK, 2 * HD), F32),
            jax.ShapeDtypeStruct((HALO, BLK, 2 * HD), BF16),
            jax.ShapeDtypeStruct((HALO, BLK, 2 * HD), BF16),
        ],
        in_specs=[smem, smem, hbm, hbm, hbm, hbm],
        out_specs=[hbm, hbm, hbm, hbm],
        scratch_shapes=[
            pltpu.VMEM((EXT, BLK, 2 * HD), BF16),
            pltpu.VMEM((GROUP, BLK, 2 * HD), BF16),
            pltpu.VMEM((EXT, BLK, 2 * HD), F32),
            pltpu.VMEM((2 * BLK, 2 * HD), BF16),
            pltpu.VMEM((SLOTS, BLK, 2 * BLK), F32),
            pltpu.VMEM((SLOTS, BLK, 2 * BLK), BF16),
            pltpu.VMEM((GROUP, BLK, HD), BF16),
            pltpu.VMEM((2 * HALO, BLK, 2 * HD), BF16),
            pltpu.SemaphoreType.DMA((4,)),
        ],
        compiler_params=pltpu.CompilerParams(vmem_limit_bytes=32 << 20),
        cost_estimate=pl.CostEstimate(
            flops=2_400_000_000, bytes_accessed=8 << 20, transcendentals=2_000_000
        ),
    )(places, live, kv, before, after, qd)


def shards(qkv, grad_out, key_lists, live_counts):
    planes = lax.axis_size("zz")
    plane = lax.axis_index("zz")
    team = ("x", "head")
    half = planes // 2
    flip = jnp.where(plane >= half, 1, 0).astype(jnp.int32).reshape(1)

    def crossing(step):
        pairs = []
        for p in range(planes):
            q = p + step
            if 0 <= q < planes:
                for r in range(RING):
                    for h in range(4):
                        other = h ^ 2 if (p >= half) != (q >= half) else h
                        pairs.append(((p * RING + r) * 4 + h, (q * RING + r) * 4 + other))
        return pairs

    everyone = ("zz", "x", "head")
    to_next = functools.partial(lax.ppermute, axis_name=everyone, perm=crossing(1))
    to_prev = functools.partial(lax.ppermute, axis_name=everyone, perm=crossing(-1))

    named = jnp.concatenate([key_lists, live_counts[:, None]], axis=1)
    ring = [named]
    for step in range(1, RING):
        ring.append(lax.ppermute(named, "x", [(i, (i + step) % RING) for i in range(RING)]))
    behind = jnp.mod(lax.axis_index("x") - jnp.arange(RING, dtype=jnp.int32), RING)
    named = jnp.take(jnp.stack(ring), behind, axis=0).reshape(GROUP, LISTED + 1)
    blocks = plane * GROUP + jnp.arange(GROUP, dtype=jnp.int32)
    window = blocks[:, None] - 1 + jnp.arange(WIN, dtype=jnp.int32)[None, :]
    window_ok = (window >= 0) & (window < planes * GROUP)
    listed_ok = jnp.arange(LISTED, dtype=jnp.int32)[None, :] < named[:, LISTED:]
    live = jnp.concatenate([window_ok, listed_ok], axis=1).astype(jnp.int32)
    places = jnp.concatenate([window, named[:, :LISTED]], axis=1) - plane * GROUP + HALO

    kv, qd = split_heads(flip, qkv, grad_out)
    kv = lax.all_to_all(kv, team, 0, 0, tiled=True)
    qd = lax.all_to_all(qd, team, 0, 0, tiled=True)
    before = to_next(kv[GROUP - HALO :])
    after = to_prev(kv[:HALO])

    dqs, dkvs = [], []
    for h in range(LOCAL):
        dq, own, tobefore, toafter = attention(h, places, live, kv, before, after, qd)
        from_next = to_prev(tobefore)
        from_prev = to_next(toafter)
        dkv = jnp.concatenate(
            [
                own[:HALO] + from_prev.astype(F32),
                own[HALO:] + from_next.astype(F32),
            ],
            axis=0,
        ).astype(BF16)
        dqs.append(dq)
        dkvs.append(dkv)
    dq = lax.all_to_all(jnp.stack(dqs, axis=1), team, 0, 0, tiled=True)
    dkv = lax.all_to_all(jnp.stack(dkvs, axis=1), team, 0, 0, tiled=True)
    return join_heads(flip, dq, dkv)


def solution(mesh):
    shape = mesh.devices.shape
    inner = Mesh(mesh.devices.reshape(shape[0] // RING, RING, shape[1]), ("zz", "x", "head"))
    everyone = ("zz", "x", "head")
    placed = (P(everyone, None), P(everyone, None), P(("zz", "x"), None), P(("zz", "x")))
    return jax.shard_map(
        shards, mesh=inner, in_specs=placed, out_specs=P(everyone, None), check_vma=False
    )
```

time: 723 us -> 203 us (0.28); the launches traced: 709 us -> 203 us
  local copies, waits for them, and re-layouts: 318 us -> 5.11 us
  waiting for transfers between devices: 150 us -> 56.4 us
  matrix products: 83.8 us -> 0 us
  Pallas kernels: 0 us -> 54.8 us
  other arithmetic: 38.5 us -> 5.12 us
  starting transfers between devices: 77.8 us -> 49.9 us
  blocking collectives: 39.4 us -> 31 us
    ppermute x16 -> x9, waiting for transfers between devices: 118 us -> 8.3 us  [the longest x1 6.18 us: shards(): before = to_next(kv[GROUP - HALO:])]
    dot_general x21 -> x0, matrix products: 74.9 us -> none  [the longest x4 28 us: shards(): jnp.einsum('st,sbf->tbf', owner_tables[side_index], arrived, precision=la...]
    reshape x5 -> x0, local copies, waits for them, and re-layouts: 73.6 us -> none  [the longest x1 51 us: shards(): flat_terms = pair_terms.reshape(slot_total, BLK * pair_width)]
    pallas_call x0 -> x4, Pallas kernels: none -> 54.8 us  [the longest x2 41.9 us: attention(): pl.pallas_call(functools.partial(attention_kernel, head), out_shape=[jax....]
    slice x14 -> x2, local copies, waits for them, and re-layouts: 50 us -> 1.65 us  [the longest x1 1.47 us: shards(): after = to_prev(kv[:HALO])]
    dynamic_update_slice x4 -> x0, local copies, waits for them, and re-layouts: 46.9 us -> none  [shards(): lax.scan(step, carry_zero, (query_blocks, grad_blocks, places, usable))]
    scatter-add x2 -> x0, local copies, waits for them, and re-layouts: 39.4 us -> none  [shards(): own_grads = own_grads.at[target_block].add(arrived)]
    ppermute x16 -> x9, starting transfers between devices: 69.8 us -> 32.8 us  [the longest x2 12.5 us: shards(): from_next = to_prev(tobefore)]
  transfers between devices with their start and end apart: 18 -> 12, of which waited for: 6 -> 6; matrix products, arithmetic and copies ran while one was open for 27% -> 4% of each run, Pallas kernels for 0% -> 10%
where the time goes in v1:
time: 203 us
  waiting for transfers between devices  56.4 us (28%)
  Pallas kernels  54.8 us (27%)
  starting transfers between devices  49.9 us (25%)
  blocking collectives  31 us (15%)
  other arithmetic  5.12 us (3%)
  local copies, waits for them, and re-layouts  5.11 us (3%)
    pallas_call x2, Pallas kernels, attention(): pl.pallas_call(functools.partial(attention_kernel, head), out_shape=[jax....  41.9 us
    all_to_all x1, blocking collectives, shards(): dkv = lax.all_to_all(jnp.stack(dkvs, axis=1), team, 0, 0, tiled=True)  31 us
    all_to_all x1, waiting for transfers between devices, shards(): kv = lax.all_to_all(kv, team, 0, 0, tiled=True)  21.4 us
    all_to_all x1, waiting for transfers between devices, shards(): qd = lax.all_to_all(qd, team, 0, 0, tiled=True)  14.5 us
    ppermute x2, starting transfers between devices, shards(): from_next = to_prev(tobefore)  12.5 us
    all_to_all x1, waiting for transfers between devices, shards(): dq = lax.all_to_all(jnp.stack(dqs, axis=1), team, 0, 0, tiled=True)  12.2 us
    all_to_all x1, starting transfers between devices, shards(): dq = lax.all_to_all(jnp.stack(dqs, axis=1), team, 0, 0, tiled=True)  7 us
    pallas_call x1, Pallas kernels, split_heads(): pl.pallas_call(send_kernel, out_shape=[parts, parts], grid_spec=pltpu.Pre...  6.61 us
  transfers between devices with their start and end apart: 12, of which 6 were waited for; matrix products, arithmetic and copies ran while one was open for 4% of the time, Pallas kernels for 10%

profile of v1, /device:TPU:16, one launch (start us, length us, event | category | flops | bytes accessed | tf_op | source)
XLA Modules:
  0.0 202.6 jit_solution(10353479784405911864)
XLA Ops:
  0.0 6.6 %shard_map.46 = (bf16[16,2,128,256]{3,2,1,0:T(8,128)(2,1)}, bf16[16,2,128,256]{3,2,1,0:T(8,128)(2,1)}) custom-call(s32[1]{0:T(128)} %bitcast.flip_ref, bf16[128,12288]{1,0:T(8,128)(2,1)} %qkv_ref.1, bf16[128,4096]{1,0:T(8,128)(2,1)} %grad_ref.1), custom_call_target="tpu_custom_call" | custom-call | bytes 8388608 | tf_op jit(solution)/shard_map/pallas_call | solution.py:47
  6.6 5.3 %all-to-all-start = ((bf16[16,2,128,256]{3,2,1,0:T(8,128)(2,1)}), bf16[16,2,128,256]{3,2,1,0:T(8,128)(2,1)S(1)}, u32[]{:S(2)}, u32[]{:S(2)}) async-start(bf16[16,2,128,256]{3,2,1,0:T(8,128)(2,1)} %get-tuple-element.15), calls=%async_computation | async-start | bytes 4194304 | tf_op jit(solution)/shard_map/all_to_all | solution.py:261
  12.1 1.9 collective-permute-start
  14.0 2.7 %collective-permute-start.1 = (s32[4,5]{1,0:T(4,128)S(1)}, s32[4,5]{1,0:T(4,128)S(1)}, u32[]{:S(2)}, u32[]{:S(2)}) collective-permute-start(s32[4,5]{1,0:T(4,128)S(1)} %pad_add_fusion.1), channel_id=1, source_target_pairs={{0,8},{4,12},{8,0},{12,4},{1,9},{5,13},{9,1},{13,5},{2,10},{6,14},... | collective-permute-start | bytes 248 | tf_op jit(solution)/shard_map/ppermute | solution.py:250
  16.7 1.5 collective-permute-start.2
  18.2 21.4 %all-to-all-done.kv_ref = bf16[16,2,128,256]{3,2,1,0:T(8,128)(2,1)S(1)} async-done(((bf16[16,2,128,256]{3,2,1,0:T(8,128)(2,1)}), bf16[16,2,128,256]{3,2,1,0:T(8,128)(2,1)S(1)}, u32[]{:S(2)}, u32[]{:S(2)}) %all-to-all-start) | async-done | bytes 2097184 | tf_op jit(solution)/shard_map/all_to_all | solution.py:261
  39.6 4.9 %all-to-all-start.1 = ((bf16[16,2,128,256]{3,2,1,0:T(8,128)(2,1)}), bf16[16,2,128,256]{3,2,1,0:T(8,128)(2,1)}, u32[]{:S(2)}, u32[]{:S(2)}) async-start(bf16[16,2,128,256]{3,2,1,0:T(8,128)(2,1)} %get-tuple-element.16), calls=%async_computation.1 | async-start | bytes 4194304 | tf_op jit(solution)/shard_map/all_to_all | solution.py:262
  44.7 1.5 fusion.8
  46.2 3.8 %collective-permute-start.3 = (bf16[8,2,128,256]{3,2,1,0:T(8,128)(2,1)}, bf16[8,2,128,256]{3,2,1,0:T(8,128)(2,1)S(1)}, u32[]{:S(2)}, u32[]{:S(2)}) collective-permute-start(bf16[8,2,128,256]{3,2,1,0:T(8,128)(2,1)} %get-tuple-element.30), channel_id=1, source_target_pairs={{0,16},{1,17},{2,18},{3,19},{4,20},{5,21},{6,22},{7,23},{8,24},{9,... | collective-permute-start | bytes 3145736 | tf_op jit(solution)/shard_map/ppermute | solution.py:263
  50.0 6.5 %collective-permute-start.4 = (bf16[8,2,128,256]{3,2,1,0:T(8,128)(2,1)}, bf16[8,2,128,256]{3,2,1,0:T(8,128)(2,1)}, u32[]{:S(2)}, u32[]{:S(2)}) collective-permute-start(bf16[8,2,128,256]{3,2,1,0:T(8,128)(2,1)} %get-tuple-element.29), channel_id=1, source_target_pairs={{16,0},{17,1},{18,2},{19,3},{20,4},{21,5},{22,6},{23,7},{24,8},{25... | collective-permute-start | bytes 3145736 | tf_op jit(solution)/shard_map/ppermute | solution.py:264
  56.8 0.6 gather_fusion
  57.5 0.2 slice_reduce_fusion
  57.8 14.5 %all-to-all-done.1.qd_ref = bf16[16,2,128,256]{3,2,1,0:T(8,128)(2,1)} async-done(((bf16[16,2,128,256]{3,2,1,0:T(8,128)(2,1)}), bf16[16,2,128,256]{3,2,1,0:T(8,128)(2,1)}, u32[]{:S(2)}, u32[]{:S(2)}) %all-to-all-start.1) | async-done | bytes 2097184 | tf_op jit(solution)/shard_map/all_to_all | solution.py:262
  72.3 6.2 %collective-permute-done.3.before_ref = bf16[8,2,128,256]{3,2,1,0:T(8,128)(2,1)S(1)} collective-permute-done((bf16[8,2,128,256]{3,2,1,0:T(8,128)(2,1)}, bf16[8,2,128,256]{3,2,1,0:T(8,128)(2,1)S(1)}, u32[]{:S(2)}, u32[]{:S(2)}) %collective-permute-start.3) | collective-permute-done | bytes 1048608 | tf_op jit(solution)/shard_map/ppermute | solution.py:263
  78.5 1.3 collective-permute-done.4.after_ref
  79.8 20.9 %shard_map.47 = (bf16[16,128,128]{2,1,0:T(8,128)(2,1)S(1)}, f32[16,128,256]{2,1,0:T(8,128)S(1)}, bf16[8,128,256]{2,1,0:T(8,128)(2,1)}, bf16[8,128,256]{2,1,0:T(8,128)(2,1)}) custom-call(s32[16,7]{1,0:T(8,128)S(1)} %fusion.4.place_ref, s32[16,7]{1,0:T(8,128)S(1)} %add_convert_fusion.4.live_ref, bf16[16,2,128,256]{3,2,1,0:T(8,128)(2,1)S(1)} %all-to-all-done.kv_ref, ...), custom_call_target="tpu_custom_call" | custom-call | flops 2400000000 | bytes 8388608 | tf_op jit(solution)/shard_map/pallas_call | solution.py:197
  100.7 1.3 copy-done.2
  102.0 1.9 collective-permute-start.5
  104.0 6.5 %collective-permute-start.6 = (bf16[8,128,256]{2,1,0:T(8,128)(2,1)}, bf16[8,128,256]{2,1,0:T(8,128)(2,1)}, u32[]{:S(2)}, u32[]{:S(2)}) collective-permute-start(bf16[8,128,256]{2,1,0:T(8,128)(2,1)} %get-tuple-element.21), channel_id=1, source_target_pairs={{16,0},{17,1},{18,2},{19,3},{20,4},{21,5},{22,6},{23,7},{24,8},{25... | collective-permute-start | bytes 1572872 | tf_op jit(solution)/shard_map/ppermute | solution.py:269
  110.5 21.0 %shard_map.48 = (bf16[16,128,128]{2,1,0:T(8,128)(2,1)S(1)}, f32[16,128,256]{2,1,0:T(8,128)S(1)}, bf16[8,128,256]{2,1,0:T(8,128)(2,1)}, bf16[8,128,256]{2,1,0:T(8,128)(2,1)}) custom-call(s32[16,7]{1,0:T(8,128)S(1)} %fusion.4.place_ref, s32[16,7]{1,0:T(8,128)S(1)} %add_convert_fusion.4.live_ref, bf16[16,2,128,256]{3,2,1,0:T(8,128)(2,1)S(1)} %all-to-all-done.kv_ref, ...), custom_call_target="tpu_custom_call" | custom-call | flops 2400000000 | bytes 8388608 | tf_op jit(solution)/shard_map/pallas_call | solution.py:197
  131.5 1.3 copy-done
  132.8 1.9 collective-permute-start.7
  134.7 6.0 %collective-permute-start.8 = (bf16[8,128,256]{2,1,0:T(8,128)(2,1)}, bf16[8,128,256]{2,1,0:T(8,128)(2,1)}, u32[]{:S(2)}, u32[]{:S(2)}) collective-permute-start(bf16[8,128,256]{2,1,0:T(8,128)(2,1)} %get-tuple-element.24), channel_id=1, source_target_pairs={{16,0},{17,1},{18,2},{19,3},{20,4},{21,5},{22,6},{23,7},{24,8},{25... | collective-permute-start | bytes 1572872 | tf_op jit(solution)/shard_map/ppermute | solution.py:269
  140.7 1.1 pad_maximum_fusion
  141.8 7.0 %all-to-all-start.2 = ((bf16[16,2,128,128]{3,2,1,0:T(8,128)(2,1)}), bf16[16,2,128,128]{3,2,1,0:T(8,128)(2,1)S(1)}, u32[]{:S(2)}, u32[]{:S(2)}) async-start(bf16[16,2,128,128]{3,2,1,0:T(8,128)(2,1)} %pad_maximum_fusion), calls=%async_computation.2 | async-start | bytes 2097152 | tf_op jit(solution)/shard_map/all_to_all | solution.py:280
  148.9 1.6 fusion
  150.5 0.8 collective-permute-done.8
  151.4 1.5 fusion.2
  152.9 0.2 maximum_maximum_fusion
  153.1 12.2 %all-to-all-done.2.dq_ref = bf16[16,2,128,128]{3,2,1,0:T(8,128)(2,1)S(1)} async-done(((bf16[16,2,128,128]{3,2,1,0:T(8,128)(2,1)}), bf16[16,2,128,128]{3,2,1,0:T(8,128)(2,1)S(1)}, u32[]{:S(2)}, u32[]{:S(2)}) %all-to-all-start.2) | async-done | bytes 1048608 | tf_op jit(solution)/shard_map/all_to_all | solution.py:280
  165.3 31.0 %all_to_all.20.dkv_ref = bf16[16,2,128,256]{3,2,1,0:T(8,128)(2,1)} all-to-all(bf16[16,2,128,256]{3,2,1,0:T(8,128)(2,1)S(1)} %maximum_maximum_fusion), channel_id=1, replica_groups=mesh['zz'=16,'x'=4,'head'=4] {'x','head'}, dimensions={0} | all-to-all | bytes 4194304 | tf_op jit(solution)/shard_map/all_to_all | solution.py:281
  196.3 6.2 %shard_map.49 = bf16[128,12288]{1,0:T(8,128)(2,1)} custom-call(s32[1]{0:T(128)} %bitcast.flip_ref, bf16[16,2,128,128]{3,2,1,0:T(8,128)(2,1)} %copy-done.4, bf16[16,2,128,256]{3,2,1,0:T(8,128)(2,1)} %all_to_all.20.dkv_ref), custom_call_target="tpu_custom_call" | custom-call | bytes 6291456 | tf_op jit(solution)/shard_map/pallas_call | solution.py:78
  (34 shorter events, 1.0 us)
Async XLA Ops:
  6.6 5.3 %copy-start.6 = (s32[4]{0:T(128)S(1)}, s32[4]{0:T(128)}, u32[]{:S(2)}) copy-start(s32[4]{0:T(128)} %param.7) | copy-start | bytes 52
  6.6 5.4 %copy-start.5 = (s32[4,4]{1,0:T(4,128)S(1)}, s32[4,4]{1,0:T(4,128)}, u32[]{:S(2)}) copy-start(s32[4,4]{1,0:T(4,128)} %param.6) | copy-start | bytes 196
  6.6 33.0 %all-to-all-start = ((bf16[16,2,128,256]{3,2,1,0:T(8,128)(2,1)}), bf16[16,2,128,256]{3,2,1,0:T(8,128)(2,1)S(1)}, u32[]{:S(2)}, u32[]{:S(2)}) async-start(bf16[16,2,128,256]{3,2,1,0:T(8,128)(2,1)} %get-tuple-element.15), calls=%async_computation | async-start | bytes 4194304 | tf_op jit(solution)/shard_map/all_to_all | solution.py:261
  12.1 44.7 %collective-permute-start = (s32[4,5]{1,0:T(4,128)S(1)}, s32[4,5]{1,0:T(4,128)S(1)}, u32[]{:S(2)}, u32[]{:S(2)}) collective-permute-start(s32[4,5]{1,0:T(4,128)S(1)} %pad_add_fusion.1), channel_id=1, source_target_pairs={{0,4},{4,8},{8,12},{12,0},{1,5},{5,9},{9,13},{13,1},{2,6},{6,10},{... | collective-permute-start | bytes 248 | tf_op jit(solution)/shard_map/ppermute | solution.py:250
  14.0 42.8 %collective-permute-start.1 = (s32[4,5]{1,0:T(4,128)S(1)}, s32[4,5]{1,0:T(4,128)S(1)}, u32[]{:S(2)}, u32[]{:S(2)}) collective-permute-start(s32[4,5]{1,0:T(4,128)S(1)} %pad_add_fusion.1), channel_id=1, source_target_pairs={{0,8},{4,12},{8,0},{12,4},{1,9},{5,13},{9,1},{13,5},{2,10},{6,14},... | collective-permute-start | bytes 248 | tf_op jit(solution)/shard_map/ppermute | solution.py:250
  16.7 40.1 %collective-permute-start.2 = (s32[4,5]{1,0:T(4,128)S(1)}, s32[4,5]{1,0:T(4,128)S(1)}, u32[]{:S(2)}, u32[]{:S(2)}) collective-permute-start(s32[4,5]{1,0:T(4,128)S(1)} %pad_add_fusion.1), channel_id=1, source_target_pairs={{0,12},{4,0},{8,4},{12,8},{1,13},{5,1},{9,5},{13,9},{2,14},{6,2},{... | collective-permute-start | bytes 248 | tf_op jit(solution)/shard_map/ppermute | solution.py:250
  39.6 32.7 %all-to-all-start.1 = ((bf16[16,2,128,256]{3,2,1,0:T(8,128)(2,1)}), bf16[16,2,128,256]{3,2,1,0:T(8,128)(2,1)}, u32[]{:S(2)}, u32[]{:S(2)}) async-start(bf16[16,2,128,256]{3,2,1,0:T(8,128)(2,1)} %get-tuple-element.16), calls=%async_computation.1 | async-start | bytes 4194304 | tf_op jit(solution)/shard_map/all_to_all | solution.py:262
  46.2 32.3 %collective-permute-start.3 = (bf16[8,2,128,256]{3,2,1,0:T(8,128)(2,1)}, bf16[8,2,128,256]{3,2,1,0:T(8,128)(2,1)S(1)}, u32[]{:S(2)}, u32[]{:S(2)}) collective-permute-start(bf16[8,2,128,256]{3,2,1,0:T(8,128)(2,1)} %get-tuple-element.30), channel_id=1, source_target_pairs={{0,16},{1,17},{2,18},{3,19},{4,20},{5,21},{6,22},{7,23},{8,24},{9,... | collective-permute-start | bytes 3145736 | tf_op jit(solution)/shard_map/ppermute | solution.py:263
  50.0 29.8 %collective-permute-start.4 = (bf16[8,2,128,256]{3,2,1,0:T(8,128)(2,1)}, bf16[8,2,128,256]{3,2,1,0:T(8,128)(2,1)}, u32[]{:S(2)}, u32[]{:S(2)}) collective-permute-start(bf16[8,2,128,256]{3,2,1,0:T(8,128)(2,1)} %get-tuple-element.29), channel_id=1, source_target_pairs={{16,0},{17,1},{18,2},{19,3},{20,4},{21,5},{22,6},{23,7},{24,8},{25... | collective-permute-start | bytes 3145736 | tf_op jit(solution)/shard_map/ppermute | solution.py:264
  100.7 1.3 copy-start.2
  102.0 46.8 %collective-permute-start.5 = (bf16[8,128,256]{2,1,0:T(8,128)(2,1)}, bf16[8,128,256]{2,1,0:T(8,128)(2,1)}, u32[]{:S(2)}, u32[]{:S(2)}) collective-permute-start(bf16[8,128,256]{2,1,0:T(8,128)(2,1)} %get-tuple-element.20), channel_id=1, source_target_pairs={{0,16},{1,17},{2,18},{3,19},{4,20},{5,21},{6,22},{7,23},{8,24},{9,... | collective-permute-start | bytes 1572872 | tf_op jit(solution)/shard_map/ppermute | solution.py:270
  104.0 44.9 %collective-permute-start.6 = (bf16[8,128,256]{2,1,0:T(8,128)(2,1)}, bf16[8,128,256]{2,1,0:T(8,128)(2,1)}, u32[]{:S(2)}, u32[]{:S(2)}) collective-permute-start(bf16[8,128,256]{2,1,0:T(8,128)(2,1)} %get-tuple-element.21), channel_id=1, source_target_pairs={{16,0},{17,1},{18,2},{19,3},{20,4},{21,5},{22,6},{23,7},{24,8},{25... | collective-permute-start | bytes 1572872 | tf_op jit(solution)/shard_map/ppermute | solution.py:269
  131.4 1.3 copy-start
  132.8 17.8 %collective-permute-start.7 = (bf16[8,128,256]{2,1,0:T(8,128)(2,1)}, bf16[8,128,256]{2,1,0:T(8,128)(2,1)}, u32[]{:S(2)}, u32[]{:S(2)}) collective-permute-start(bf16[8,128,256]{2,1,0:T(8,128)(2,1)} %get-tuple-element.23), channel_id=1, source_target_pairs={{0,16},{1,17},{2,18},{3,19},{4,20},{5,21},{6,22},{7,23},{8,24},{9,... | collective-permute-start | bytes 1572872 | tf_op jit(solution)/shard_map/ppermute | solution.py:270
  134.7 16.7 %collective-permute-start.8 = (bf16[8,128,256]{2,1,0:T(8,128)(2,1)}, bf16[8,128,256]{2,1,0:T(8,128)(2,1)}, u32[]{:S(2)}, u32[]{:S(2)}) collective-permute-start(bf16[8,128,256]{2,1,0:T(8,128)(2,1)} %get-tuple-element.24), channel_id=1, source_target_pairs={{16,0},{17,1},{18,2},{19,3},{20,4},{21,5},{22,6},{23,7},{24,8},{25... | collective-permute-start | bytes 1572872 | tf_op jit(solution)/shard_map/ppermute | solution.py:269
  140.7 8.1 %copy-start.3 = (f32[16,128,256]{2,1,0:T(8,128)S(1)}, f32[16,128,256]{2,1,0:T(8,128)}, u32[]{:S(2)}) copy-start(f32[16,128,256]{2,1,0:T(8,128)} %copy-done.2) | copy-start | bytes 6291460
  141.8 23.5 %all-to-all-start.2 = ((bf16[16,2,128,128]{3,2,1,0:T(8,128)(2,1)}), bf16[16,2,128,128]{3,2,1,0:T(8,128)(2,1)S(1)}, u32[]{:S(2)}, u32[]{:S(2)}) async-start(bf16[16,2,128,128]{3,2,1,0:T(8,128)(2,1)} %pad_maximum_fusion), calls=%async_computation.2 | async-start | bytes 2097152 | tf_op jit(solution)/shard_map/all_to_all | solution.py:280
  148.9 2.5 %copy-start.1 = (f32[16,128,256]{2,1,0:T(8,128)S(1)}, f32[16,128,256]{2,1,0:T(8,128)}, u32[]{:S(2)}) copy-start(f32[16,128,256]{2,1,0:T(8,128)} %copy-done) | copy-start | bytes 6291460
  165.3 31.0 %copy-start.4 = (bf16[16,2,128,128]{3,2,1,0:T(8,128)(2,1)}, bf16[16,2,128,128]{3,2,1,0:T(8,128)(2,1)S(1)}, u32[]{:S(2)}) copy-start(bf16[16,2,128,128]{3,2,1,0:T(8,128)(2,1)S(1)} %all-to-all-done.2.dq_ref) | copy-start | bytes 3145732

commit v2 on v1

v2 whole, which is shorter than its diff:
```python
import functools

import jax
import jax.numpy as jnp
from jax import lax
from jax.experimental import pallas as pl
from jax.experimental.pallas import tpu as pltpu
from jax.sharding import Mesh
from jax.sharding import PartitionSpec as P

HD = 128
BLK = 128
TILES = 4
SPAN = 2
LISTED = 4
WIN = 3
RING = 4
GROUP = RING * TILES
HALO = SPAN * TILES
EXT = GROUP + 2 * HALO
LOCAL = 2
SLOTS = WIN + LISTED
COLS = LOCAL * 3 * HD
LOG2E = 1.4426950408889634
F32 = jnp.float32
BF16 = jnp.bfloat16


VMEM = pl.BlockSpec(memory_space=pltpu.VMEM)
SMEM = pl.BlockSpec(memory_space=pltpu.SMEM)
HBM = pl.BlockSpec(memory_space=pl.ANY)


def run_all(pairs, sem):
    running = [pltpu.make_async_copy(s, d, sem.at[i]) for i, (s, d) in enumerate(pairs)]
    for c in running:
        c.start()
    for c in running:
        c.wait()


def columns(part, flip, head):
    pair = (part // 4) * 4 + jnp.bitwise_xor(part % 4, flip)
    at = pair * LOCAL + head
    return pl.multiple_of(at * 3 * HD, 3 * HD), pl.multiple_of(at * HD, HD)


def send_pairs_kernel(flip_ref, qkv_ref, kv_ref, sem):
    pairs = []
    for part in range(GROUP):
        for h in range(LOCAL):
            at, _ = columns(part, flip_ref[0], h)
            pairs.append((qkv_ref.at[:, pl.ds(at + HD, 2 * HD)], kv_ref.at[part, h]))
    run_all(pairs, sem)


def send_pairs(flip, qkv):
    return pl.pallas_call(
        send_pairs_kernel,
        out_shape=jax.ShapeDtypeStruct((GROUP, LOCAL, BLK, 2 * HD), BF16),
        in_specs=[SMEM, HBM],
        out_specs=VMEM,
        scratch_shapes=[pltpu.SemaphoreType.DMA((GROUP * LOCAL,))],
        compiler_params=pltpu.CompilerParams(vmem_limit_bytes=8 << 20),
        cost_estimate=pl.CostEstimate(flops=0, bytes_accessed=4 << 20, transcendentals=0),
    )(flip, qkv)


def send_queries_kernel(flip_ref, qkv_ref, grad_ref, qd0_ref, qd1_ref, sem):
    pairs = []
    for part in range(GROUP):
        for h, qd_ref in enumerate((qd0_ref, qd1_ref)):
            at, gat = columns(part, flip_ref[0], h)
            pairs.append((qkv_ref.at[:, pl.ds(at, HD)], qd_ref.at[part, :, pl.ds(0, HD)]))
            pairs.append((grad_ref.at[:, pl.ds(gat, HD)], qd_ref.at[part, :, pl.ds(HD, HD)]))
    run_all(pairs, sem)


def send_queries(flip, qkv, grad_out):
    part = jax.ShapeDtypeStruct((GROUP, BLK, 2 * HD), BF16)
    return pl.pallas_call(
        send_queries_kernel,
        out_shape=[part, part],
        in_specs=[SMEM, HBM, HBM],
        out_specs=[VMEM, VMEM],
        scratch_shapes=[pltpu.SemaphoreType.DMA((GROUP * LOCAL * 2,))],
        compiler_params=pltpu.CompilerParams(vmem_limit_bytes=8 << 20),
        cost_estimate=pl.CostEstimate(flops=0, bytes_accessed=4 << 20, transcendentals=0),
    )(flip, qkv, grad_out)


def join_early_kernel(flip_ref, dq0_ref, mid_ref, out_ref, sem):
    pairs = []
    for part in range(GROUP):
        at0, _ = columns(part, flip_ref[0], 0)
        at1, _ = columns(part, flip_ref[0], 1)
        pairs.append((dq0_ref.at[part], out_ref.at[:, pl.ds(at0, HD)]))
        pairs.append((mid_ref.at[part, :, pl.ds(0, HD)], out_ref.at[:, pl.ds(at1, HD)]))
        pairs.append(
            (mid_ref.at[part, :, pl.ds(HD, 2 * HD)], out_ref.at[:, pl.ds(at0 + HD, 2 * HD)])
        )
    run_all(pairs, sem)


def join_early(flip, dq0, mid):
    return pl.pallas_call(
        join_early_kernel,
        out_shape=jax.ShapeDtypeStruct((BLK, GROUP * COLS), BF16),
        in_specs=[SMEM, VMEM, VMEM],
        out_specs=HBM,
        scratch_shapes=[pltpu.SemaphoreType.DMA((GROUP * 3,))],
        compiler_params=pltpu.CompilerParams(vmem_limit_bytes=8 << 20),
        cost_estimate=pl.CostEstimate(flops=0, bytes_accessed=4 << 20, transcendentals=0),
    )(flip, dq0, mid)


def join_late_kernel(flip_ref, dkv_ref, held_ref, out_ref, sem):
    pairs = []
    for part in range(GROUP):
        at, _ = columns(part, flip_ref[0], 1)
        pairs.append((dkv_ref.at[part], out_ref.at[:, pl.ds(at + HD, 2 * HD)]))
    run_all(pairs, sem)


def join_late(flip, dkv, held):
    return pl.pallas_call(
        join_late_kernel,
        out_shape=jax.ShapeDtypeStruct((BLK, GROUP * COLS), BF16),
        in_specs=[SMEM, VMEM, HBM],
        out_specs=HBM,
        scratch_shapes=[pltpu.SemaphoreType.DMA((GROUP,))],
        input_output_aliases={2: 0},
        compiler_params=pltpu.CompilerParams(vmem_limit_bytes=8 << 20),
        cost_estimate=pl.CostEstimate(flops=0, bytes_accessed=2 << 20, transcendentals=0),
    )(flip, dkv, held)


def add_kernel(acc_ref, prev_ref, next_ref, *refs):
    out_ref = refs[-1]
    left = 0
    if len(refs) == 2:
        out_ref[:, :, 0:HD] = refs[0][...]
        left = HD
    for b in range(GROUP):
        more = prev_ref[b] if b < HALO else next_ref[b - HALO]
        sums = acc_ref[b]
        dk = sums[:, 0:HD] * (HD ** (-0.5)) + more[:, 0:HD].astype(F32)
        dv = sums[:, HD : 2 * HD] + more[:, HD : 2 * HD].astype(F32)
        out_ref[b, :, left : left + HD] = dk.astype(BF16)
        out_ref[b, :, left + HD : left + 2 * HD] = dv.astype(BF16)


def add_halo(acc, from_prev, from_next, *dq):
    width = (3 if dq else 2) * HD
    return pl.pallas_call(
        add_kernel,
        out_shape=jax.ShapeDtypeStruct((GROUP, BLK, width), BF16),
        in_specs=[VMEM] * (3 + len(dq)),
        out_specs=VMEM,
        compiler_params=pltpu.CompilerParams(vmem_limit_bytes=12 << 20),
        cost_estimate=pl.CostEstimate(flops=2 << 20, bytes_accessed=4 << 20, transcendentals=0),
    )(acc, from_prev, from_next, *dq)


def attention_kernel(
    head,
    place_ref,
    live_ref,
    kv_ref,
    before_ref,
    after_ref,
    qd,
    dq_ref,
    own_ref,
    tobefore_ref,
    toafter_ref,
    kv,
    acc,
    mix,
    chosen,
    tall,
    low,
    dqs,
    outs,
    sem,
):
    loads = [
        pltpu.make_async_copy(before_ref, kv.at[pl.ds(0, HALO)], sem.at[0]),
        pltpu.make_async_copy(kv_ref.at[:, head], kv.at[pl.ds(HALO, GROUP)], sem.at[1]),
        pltpu.make_async_copy(after_ref, kv.at[pl.ds(HALO + GROUP, HALO)], sem.at[2]),
    ]
    for c in loads:
        c.start()
    acc[...] = jnp.zeros_like(acc)
    mix[...] = jnp.zeros_like(mix)
    for c in loads:
        c.wait()
    scale = HD ** (-0.5)

    def begin(block, side):
        mix[side, 0:BLK, 0:HD] = qd[block, :, 0:HD]
        mix[side, BLK : 2 * BLK, HD : 2 * HD] = qd[block, :, HD : 2 * HD]
        for j in range(SLOTS):
            chosen[side, j * BLK : (j + 1) * BLK] = kv[place_ref[block, j]]
        tall[side] = lax.dot_general(
            chosen[side], mix[side], (((1,), (1,)), ((), ())), preferred_element_type=F32
        )

    def middle(block, side):
        high = jnp.full((8, BLK), -3e38, F32)
        biases = [jnp.where(live_ref[block, j] > 0, 0.0, -1e30).astype(F32) for j in range(SLOTS)]
        for j in range(SLOTS):
            scores = tall[side, j * BLK : (j + 1) * BLK, 0:BLK] * (scale * LOG2E) + biases[j]
            high = jnp.maximum(high, jnp.max(scores.reshape(BLK // 8, 8, BLK), axis=0))
        top = jnp.max(high, axis=0, keepdims=True)
        total = jnp.zeros((8, BLK), F32)
        cross = jnp.zeros((8, BLK), F32)
        for j in range(SLOTS):
            rows = slice(j * BLK, (j + 1) * BLK)
            powers = jnp.exp2(tall[side, rows, 0:BLK] * (scale * LOG2E) + (biases[j] - top))
            tall[side, rows, 0:BLK] = powers
            total = total + jnp.sum(powers.reshape(BLK // 8, 8, BLK), axis=0)
            cross = cross + jnp.sum(
                (powers * tall[side, rows, BLK : 2 * BLK]).reshape(BLK // 8, 8, BLK), axis=0
            )
        inverse = 1.0 / jnp.sum(total, axis=0, keepdims=True)
        delta = jnp.sum(cross, axis=0, keepdims=True) * inverse
        for j in range(SLOTS):
            rows = slice(j * BLK, (j + 1) * BLK)
            soft = tall[side, rows, 0:BLK] * inverse
            low[side, rows, 0:BLK] = (soft * (tall[side, rows, BLK : 2 * BLK] - delta)).astype(BF16)
            low[side, rows, BLK : 2 * BLK] = soft.astype(BF16)

    def end(block, side):
        grad_query = lax.dot_general(
            low[side, :, 0:BLK], chosen[side, :, 0:HD], (((0,), (0,)), ((), ())), preferred_element_type=F32
        )
        dqs[block] = (grad_query * scale).astype(BF16)
        back = lax.dot_general(
            low[side], mix[side], (((1,), (0,)), ((), ())), preferred_element_type=F32
        )
        for j in range(SLOTS):
            acc[place_ref[block, j]] += back[j * BLK : (j + 1) * BLK]

    def step(i, _):
        for k in range(4):
            begin(4 * i + k, k)
        for k in range(4):
            middle(4 * i + k, k)
        for k in range(4):
            end(4 * i + k, k)
        return 0

    lax.fori_loop(0, GROUP // 4, step, 0)

    column = lax.broadcasted_iota(jnp.int32, (1, 1, 2 * HD), 2)
    factor = jnp.where(column < HD, scale, 1.0).astype(F32)
    stores = [
        pltpu.make_async_copy(dqs, dq_ref, sem.at[0]),
        pltpu.make_async_copy(acc.at[pl.ds(HALO, GROUP)], own_ref, sem.at[1]),
        pltpu.make_async_copy(outs.at[pl.ds(0, HALO)], tobefore_ref, sem.at[2]),
        pltpu.make_async_copy(outs.at[pl.ds(HALO, HALO)], toafter_ref, sem.at[3]),
    ]
    for c in stores[:2]:
        c.start()
    outs[0:HALO] = (acc[0:HALO] * factor).astype(BF16)
    outs[HALO : 2 * HALO] = (acc[HALO + GROUP : EXT] * factor).astype(BF16)
    for c in stores[2:]:
        c.start()
    for c in stores:
        c.wait()


def attention(head, places, live, kv, before, after, qd):
    return pl.pallas_call(
        functools.partial(attention_kernel, head),
        out_shape=[
            jax.ShapeDtypeStruct((GROUP, BLK, HD), BF16),
            jax.ShapeDtypeStruct((GROUP, BLK, 2 * HD), F32),
            jax.ShapeDtypeStruct((HALO, BLK, 2 * HD), BF16),
            jax.ShapeDtypeStruct((HALO, BLK, 2 * HD), BF16),
        ],
        in_specs=[SMEM, SMEM, HBM, HBM, HBM, VMEM],
        out_specs=[HBM] * 4,
        scratch_shapes=[
            pltpu.VMEM((EXT, BLK, 2 * HD), BF16),
            pltpu.VMEM((EXT, BLK, 2 * HD), F32),
            pltpu.VMEM((4, 2 * BLK, 2 * HD), BF16),
            pltpu.VMEM((4, SLOTS * BLK, 2 * HD), BF16),
            pltpu.VMEM((4, SLOTS * BLK, 2 * BLK), F32),
            pltpu.VMEM((4, SLOTS * BLK, 2 * BLK), BF16),
            pltpu.VMEM((GROUP, BLK, HD), BF16),
            pltpu.VMEM((2 * HALO, BLK, 2 * HD), BF16),
            pltpu.SemaphoreType.DMA((4,)),
        ],
        compiler_params=pltpu.CompilerParams(vmem_limit_bytes=20 << 20),
        cost_estimate=pl.CostEstimate(
            flops=2_400_000_000, bytes_accessed=8 << 20, transcendentals=2_000_000
        ),
    )(places, live, kv, before, after, qd)


def shards(qkv, grad_out, key_lists, live_counts):
    planes = lax.axis_size("zz")
    plane = lax.axis_index("zz")
    team = ("x", "head")
    half = planes // 2
    flip = jnp.where(plane >= half, 2, 0).astype(jnp.int32).reshape(1)

    def crossing(step):
        pairs = []
        for p in range(planes):
            q = p + step
            if 0 <= q < planes:
                for r in range(RING):
                    for h in range(4):
                        other = h ^ 2 if (p >= half) != (q >= half) else h
                        pairs.append(((p * RING + r) * 4 + h, (q * RING + r) * 4 + other))
        return pairs

    everyone = ("zz", "x", "head")
    to_next = functools.partial(lax.ppermute, axis_name=everyone, perm=crossing(1))
    to_prev = functools.partial(lax.ppermute, axis_name=everyone, perm=crossing(-1))

    named = jnp.concatenate([key_lists, live_counts[:, None]], axis=1)
    ring = [named]
    for step in range(1, RING):
        ring.append(lax.ppermute(named, "x", [(i, (i + step) % RING) for i in range(RING)]))
    behind = jnp.mod(lax.axis_index("x") - jnp.arange(RING, dtype=jnp.int32), RING)
    named = jnp.take(jnp.stack(ring), behind, axis=0).reshape(GROUP, LISTED + 1)
    blocks = plane * GROUP + jnp.arange(GROUP, dtype=jnp.int32)
    window = blocks[:, None] - 1 + jnp.arange(WIN, dtype=jnp.int32)[None, :]
    window_ok = (window >= 0) & (window < planes * GROUP)
    listed_ok = jnp.arange(LISTED, dtype=jnp.int32)[None, :] < named[:, LISTED:]
    live = jnp.concatenate([window_ok, listed_ok], axis=1).astype(jnp.int32)
    places = jnp.concatenate([window, named[:, :LISTED]], axis=1) - plane * GROUP + HALO

    swap = functools.partial(lax.all_to_all, axis_name=team, split_axis=0, concat_axis=0, tiled=True)
    qd0, qd1 = send_queries(flip, qkv, grad_out)
    kv = swap(send_pairs(flip, qkv))
    kv, qd0 = lax.optimization_barrier((kv, qd0))
    halo0 = (to_next(kv[GROUP - HALO :, 0]), to_prev(kv[:HALO, 0]))
    qd0, halo0, qd1, edge1 = lax.optimization_barrier(
        (swap(qd0), halo0, qd1, (kv[GROUP - HALO :, 1], kv[:HALO, 1]))
    )
    halos = (halo0, (to_next(edge1[0]), to_prev(edge1[1])))
    qds = (qd0, swap(qd1))

    dq0, acc0, tobefore0, toafter0 = attention(0, places, live, kv, *halos[0], qds[0])
    back0 = (to_next(toafter0), to_prev(tobefore0))
    dq1, acc1, tobefore1, toafter1 = attention(1, places, live, kv, *halos[1], qds[1])
    back1 = (to_next(toafter1), to_prev(tobefore1))
    dq0 = swap(dq0)
    mid = swap(add_halo(acc0, *back0, dq1))
    held = join_early(flip, dq0, mid)
    dkv1 = swap(add_halo(acc1, *back1))
    return join_late(flip, dkv1, held)


def solution(mesh):
    shape = mesh.devices.shape
    inner = Mesh(mesh.devices.reshape(shape[0] // RING, RING, shape[1]), ("zz", "x", "head"))
    everyone = ("zz", "x", "head")
    placed = (P(everyone, None), P(everyone, None), P(("zz", "x"), None), P(("zz", "x")))
    return jax.shard_map(
        shards, mesh=inner, in_specs=placed, out_specs=P(everyone, None), check_vma=False
    )
```

time: 203 us -> 183 us (0.901)
  blocking collectives: 31 us -> 0 us
  starting transfers between devices: 49.9 us -> 74.7 us
  Pallas kernels: 54.8 us -> 35.3 us
  local copies, waits for them, and re-layouts: 5.11 us -> 16.6 us
  other arithmetic: 5.12 us -> 0.65 us
    all_to_all x1 -> x0, blocking collectives: 31 us -> none  [shards(): dkv = lax.all_to_all(jnp.stack(dkvs, axis=1), team, 0, 0, tiled=True)]
    all_to_all x3 -> x6, starting transfers between devices: 17.2 us -> 34.4 us  [the longest x1 6.64 us: shards(): dkv1 = swap(add_halo(acc1, *back1))]
    pallas_call x2, Pallas kernels: 41.9 us -> 25.3 us  [attention(): pl.pallas_call(functools.partial(attention_kernel, head), out_shape=[jax....]
    all_to_all x3 -> x6, waiting for transfers between devices: 48.1 us -> 32.8 us  [the longest x1 18 us: shards(): kv = swap(send_pairs(flip, qkv))]
    ppermute x6 -> x8, waiting for transfers between devices: 8.29 us -> 22 us  [the longest x2 11.5 us: shards(): back1 = (to_next(toafter1), to_prev(tobefore1))]
    unnamed x14 -> x36, local copies, waits for them, and re-layouts: 2.63 us -> 12.8 us
    ppermute x6 -> x8, starting transfers between devices: 26.7 us -> 35.5 us  [the longest x2 10.2 us: shards(): halo0 = (to_next(kv[GROUP - HALO:, 0]), to_prev(kv[:HALO, 0]))]
    concatenate x2 -> x0, other arithmetic: 3.18 us -> none  [shards(): jnp.concatenate([own[:HALO] + from_prev.astype(F32), own[HALO:] + from_ne...]
  transfers between devices with their start and end apart: 12 -> 17, of which waited for: 6 -> 6; matrix products, arithmetic and copies ran while one was open for 4% -> 2% of each run, Pallas kernels for 10% -> 18%
where the time goes in v2:
time: 183 us; the launch traced here: 182 us
  starting transfers between devices  74.7 us (41%)
  waiting for transfers between devices  54.8 us (30%)
  Pallas kernels  35.3 us (19%)
  local copies, waits for them, and re-layouts  16.6 us (9%)
    pallas_call x2, Pallas kernels, attention(): pl.pallas_call(functools.partial(attention_kernel, head), out_shape=[jax....  25.3 us
    all_to_all x1, waiting for transfers between devices, shards(): kv = swap(send_pairs(flip, qkv))  18 us
    all_to_all x1, waiting for transfers between devices, shards(): dkv1 = swap(add_halo(acc1, *back1))  14.8 us
    unnamed x36, local copies, waits for them, and re-layouts  12.8 us
    ppermute x2, waiting for transfers between devices, shards(): back1 = (to_next(toafter1), to_prev(tobefore1))  11.5 us
    ppermute x2, waiting for transfers between devices, shards(): halo0 = (to_next(kv[GROUP - HALO:, 0]), to_prev(kv[:HALO, 0]))  10.6 us
    ppermute x2, starting transfers between devices, shards(): halo0 = (to_next(kv[GROUP - HALO:, 0]), to_prev(kv[:HALO, 0]))  10.2 us
    ppermute x2, starting transfers between devices, shards(): halos = (halo0, (to_next(edge1[0]), to_prev(edge1[1])))  9.44 us
  transfers between devices with their start and end apart: 17, of which 6 were waited for; matrix products, arithmetic and copies ran while one was open for 2% of the time, Pallas kernels for 18%

profile of v2, /device:TPU:16, one launch (start us, length us, event | category | flops | bytes accessed | tf_op | source)
XLA Modules:
  0.0 182.3 jit_solution(7953286699779880855)
XLA Ops:
  0.0 1.9 %copy-done = bf16[128,12288]{1,0:T(8,128)(2,1)S(1)} copy-done((bf16[128,12288]{1,0:T(8,128)(2,1)S(1)}, bf16[128,12288]{1,0:T(8,128)(2,1)}, u32[]{:S(2)}) %copy-start) | copy-done | bytes 3145752
  2.7 1.3 copy-done.2
  4.0 5.4 %all-to-all-start = ((bf16[16,2,128,256]{3,2,1,0:T(8,128)(2,1)}), bf16[16,2,128,256]{3,2,1,0:T(8,128)(2,1)}, u32[]{:S(2)}, u32[]{:S(2)}) async-start(bf16[16,2,128,256]{3,2,1,0:T(8,128)(2,1)} %copy-done.2), calls=%async_computation | async-start | bytes 4194304 | tf_op jit(solution)/shard_map/all_to_all | solution.py:340
  9.6 3.1 %collective-permute-start.2 = (s32[4,5]{1,0:T(4,128)S(1)}, s32[4,5]{1,0:T(4,128)S(1)}, u32[]{:S(2)}, u32[]{:S(2)}) collective-permute-start(s32[4,5]{1,0:T(4,128)S(1)} %pad_add_fusion.1), channel_id=1, source_target_pairs={{0,12},{4,0},{8,4},{12,8},{1,13},{5,1},{9,5},{13,9},{2,14},{6,2},{... | collective-permute-start | bytes 248 | tf_op jit(solution)/shard_map/ppermute | solution.py:328
  14.4 1.2 copy-done.5
  15.6 2.5 %shard_map.47 = (bf16[16,128,256]{2,1,0:T(8,128)(2,1)S(1)}, bf16[16,128,256]{2,1,0:T(8,128)(2,1)}) custom-call(s32[1]{0:T(128)} %bitcast.flip_ref, bf16[128,12288]{1,0:T(8,128)(2,1)S(1)} %copy-done.1, bf16[128,4096]{1,0:T(8,128)(2,1)S(1)} %copy-done.5), custom_call_target="tpu_custom_call" | custom-call | bytes 4194304 | tf_op jit(solution)/shard_map/pallas_call | solution.py:81
  19.2 18.0 %all-to-all-done.kv_ref = bf16[16,2,128,256]{3,2,1,0:T(8,128)(2,1)} async-done(((bf16[16,2,128,256]{3,2,1,0:T(8,128)(2,1)}), bf16[16,2,128,256]{3,2,1,0:T(8,128)(2,1)}, u32[]{:S(2)}, u32[]{:S(2)}) %all-to-all-start) | async-done | bytes 2097184 | tf_op jit(solution)/shard_map/all_to_all | solution.py:340
  37.2 4.8 %all-to-all-start.1 = ((bf16[16,128,256]{2,1,0:T(8,128)(2,1)}), bf16[16,128,256]{2,1,0:T(8,128)(2,1)S(1)}, u32[]{:S(2)}, u32[]{:S(2)}) async-start(bf16[16,128,256]{2,1,0:T(8,128)(2,1)} %copy-done.6), calls=%async_computation.1 | async-start | bytes 2097152 | tf_op jit(solution)/shard_map/all_to_all | solution.py:344
  42.1 2.7 %slice_bitcast_fusion = (bf16[8,128,256]{2,1,0:T(8,128)(2,1)}, bf16[8,128,256]{2,1,0:T(8,128)(2,1)}, bf16[8,128,256]{2,1,0:T(8,128)(2,1)S(1)}, bf16[8,128,256]{2,1,0:T(8,128)(2,1)S(1)}) fusion(bf16[16,2,128,256]{3,2,1,0:T(8,128)(2,1)} %all-to-all-done.kv_ref), kind=kLoop, calls=%fused_computation.1 | loop fusion | bytes 4194304 | tf_op jit(solution)/shard_map/squeeze | solution.py:344
  44.8 3.8 %collective-permute-start.3 = (bf16[8,128,256]{2,1,0:T(8,128)(2,1)S(1)}, bf16[8,128,256]{2,1,0:T(8,128)(2,1)S(1)}, u32[]{:S(2)}, u32[]{:S(2)}) collective-permute-start(bf16[8,128,256]{2,1,0:T(8,128)(2,1)S(1)} %get-tuple-element.44), channel_id=1, source_target_pairs={{0,16},{1,17},{2,18},{3,19},{4,20},{5,21},{6,22},{7,23},{8,24},{9,... | collective-permute-start | bytes 1572872 | tf_op jit(solution)/shard_map/ppermute | solution.py:342
  48.6 6.4 %collective-permute-start.4 = (bf16[8,128,256]{2,1,0:T(8,128)(2,1)S(1)}, bf16[8,128,256]{2,1,0:T(8,128)(2,1)S(1)}, u32[]{:S(2)}, u32[]{:S(2)}) collective-permute-start(bf16[8,128,256]{2,1,0:T(8,128)(2,1)S(1)} %get-tuple-element.43), channel_id=1, source_target_pairs={{16,0},{17,1},{18,2},{19,3},{20,4},{21,5},{22,6},{23,7},{24,8},{25... | collective-permute-start | bytes 1572872 | tf_op jit(solution)/shard_map/ppermute | solution.py:342
  55.9 9.4 %collective-permute-done.3.before_ref = bf16[8,128,256]{2,1,0:T(8,128)(2,1)S(1)} collective-permute-done((bf16[8,128,256]{2,1,0:T(8,128)(2,1)S(1)}, bf16[8,128,256]{2,1,0:T(8,128)(2,1)S(1)}, u32[]{:S(2)}, u32[]{:S(2)}) %collective-permute-start.3) | collective-permute-done | bytes 524320 | tf_op jit(solution)/shard_map/ppermute | solution.py:342
  66.5 5.0 %all-to-all-start.2 = ((bf16[16,128,256]{2,1,0:T(8,128)(2,1)}), bf16[16,128,256]{2,1,0:T(8,128)(2,1)}, u32[]{:S(2)}, u32[]{:S(2)}) async-start(bf16[16,128,256]{2,1,0:T(8,128)(2,1)} %get-tuple-element.29), calls=%async_computation.2 | async-start | bytes 2097152 | tf_op jit(solution)/shard_map/all_to_all | solution.py:347
  72.0 2.5 %collective-permute-start.5 = (bf16[8,128,256]{2,1,0:T(8,128)(2,1)}, bf16[8,128,256]{2,1,0:T(8,128)(2,1)}, u32[]{:S(2)}, u32[]{:S(2)}) collective-permute-start(bf16[8,128,256]{2,1,0:T(8,128)(2,1)} %get-tuple-element.27), channel_id=1, source_target_pairs={{0,16},{1,17},{2,18},{3,19},{4,20},{5,21},{6,22},{7,23},{8,24},{9,... | collective-permute-start | bytes 1572872 | tf_op jit(solution)/shard_map/ppermute | solution.py:346
  74.5 6.9 %collective-permute-start.6 = (bf16[8,128,256]{2,1,0:T(8,128)(2,1)}, bf16[8,128,256]{2,1,0:T(8,128)(2,1)}, u32[]{:S(2)}, u32[]{:S(2)}) collective-permute-start(bf16[8,128,256]{2,1,0:T(8,128)(2,1)} %get-tuple-element.28), channel_id=1, source_target_pairs={{16,0},{17,1},{18,2},{19,3},{20,4},{21,5},{22,6},{23,7},{24,8},{25... | collective-permute-start | bytes 1572872 | tf_op jit(solution)/shard_map/ppermute | solution.py:346
  83.6 12.8 %shard_map.50 = (bf16[16,128,128]{2,1,0:T(8,128)(2,1)S(1)}, f32[16,128,256]{2,1,0:T(8,128)S(1)}, bf16[8,128,256]{2,1,0:T(8,128)(2,1)}, bf16[8,128,256]{2,1,0:T(8,128)(2,1)}) custom-call(s32[16,7]{1,0:T(8,128)S(1)} %fusion.place_ref, s32[16,7]{1,0:T(8,128)S(1)} %add_convert_fusion.live_ref, bf16[16,2,128,256]{3,2,1,0:T(8,128)(2,1)} %all-to-all-done.kv_ref, ...), custom_call_target="tpu_custom_call" | custom-call | flops 2400000000 | bytes 8388608 | tf_op jit(solution)/shard_map/pallas_call | solution.py:275
  97.1 1.9 %collective-permute-start.9 = (bf16[8,128,256]{2,1,0:T(8,128)(2,1)}, bf16[8,128,256]{2,1,0:T(8,128)(2,1)}, u32[]{:S(2)}, u32[]{:S(2)}) collective-permute-start(bf16[8,128,256]{2,1,0:T(8,128)(2,1)} %get-tuple-element.38), channel_id=1, source_target_pairs={{0,16},{1,17},{2,18},{3,19},{4,20},{5,21},{6,22},{7,23},{8,24},{9,... | collective-permute-start | bytes 1572872 | tf_op jit(solution)/shard_map/ppermute | solution.py:350
  99.1 6.0 %collective-permute-start.10 = (bf16[8,128,256]{2,1,0:T(8,128)(2,1)}, bf16[8,128,256]{2,1,0:T(8,128)(2,1)}, u32[]{:S(2)}, u32[]{:S(2)}) collective-permute-start(bf16[8,128,256]{2,1,0:T(8,128)(2,1)} %get-tuple-element.39), channel_id=1, source_target_pairs={{16,0},{17,1},{18,2},{19,3},{20,4},{21,5},{22,6},{23,7},{24,8},{25... | collective-permute-start | bytes 1572872 | tf_op jit(solution)/shard_map/ppermute | solution.py:350
  105.1 6.6 %all-to-all-start.4 = ((bf16[16,128,128]{2,1,0:T(8,128)(2,1)}), bf16[16,128,128]{2,1,0:T(8,128)(2,1)S(1)}, u32[]{:S(2)}, u32[]{:S(2)}) async-start(bf16[16,128,128]{2,1,0:T(8,128)(2,1)} %copy-done.7), calls=%async_computation.4 | async-start | bytes 1048576 | tf_op jit(solution)/shard_map/all_to_all | solution.py:353
  111.7 12.6 %shard_map.48 = (bf16[16,128,128]{2,1,0:T(8,128)(2,1)S(1)}, f32[16,128,256]{2,1,0:T(8,128)S(1)}, bf16[8,128,256]{2,1,0:T(8,128)(2,1)S(1)}, bf16[8,128,256]{2,1,0:T(8,128)(2,1)S(1)}) custom-call(s32[16,7]{1,0:T(8,128)S(1)} %fusion.place_ref, s32[16,7]{1,0:T(8,128)S(1)} %add_convert_fusion.live_ref, bf16[16,2,128,256]{3,2,1,0:T(8,128)(2,1)} %all-to-all-done.kv_ref, ...), custom_call_target="tpu_custom_call" | custom-call | flops 2400000000 | bytes 8388608 | tf_op jit(solution)/shard_map/pallas_call | solution.py:275
  124.3 1.3 copy-done.3
  127.3 2.7 %shard_map.51 = bf16[16,128,384]{2,1,0:T(8,128)(2,1)} custom-call(f32[16,128,256]{2,1,0:T(8,128)S(1)} %get-tuple-element.37.acc_ref, bf16[8,128,256]{2,1,0:T(8,128)(2,1)} %collective-permute-done.9.prev_ref, bf16[8,128,256]{2,1,0:T(8,128)(2,1)} %collective-permute-done.10.next_ref, bf16[16,128,128]{2,1,0:T(8,128)(2,1)S(1)} %get-tuple-element.40.refs_0_), custom_call_target="tpu_custom_call" | custom-call | flops 2097152 | bytes 4194304 | tf_op jit(solution)/shard_map/pallas_call | solution.py:155
  130.0 5.9 %all-to-all-start.5 = ((bf16[16,128,384]{2,1,0:T(8,128)(2,1)}), bf16[16,128,384]{2,1,0:T(8,128)(2,1)S(1)}, u32[]{:S(2)}, u32[]{:S(2)}) async-start(bf16[16,128,384]{2,1,0:T(8,128)(2,1)} %shard_map.51), calls=%async_computation.5 | async-start | bytes 3145728 | tf_op jit(solution)/shard_map/all_to_all | solution.py:354
  135.9 1.9 %collective-permute-start.7 = (bf16[8,128,256]{2,1,0:T(8,128)(2,1)S(1)}, bf16[8,128,256]{2,1,0:T(8,128)(2,1)S(1)}, u32[]{:S(2)}, u32[]{:S(2)}) collective-permute-start(bf16[8,128,256]{2,1,0:T(8,128)(2,1)S(1)} %copy-done.15), channel_id=1, source_target_pairs={{0,16},{1,17},{2,18},{3,19},{4,20},{5,21},{6,22},{7,23},{8,24},{9,... | collective-permute-start | bytes 1572872 | tf_op jit(solution)/shard_map/ppermute | solution.py:352
  137.8 6.0 %collective-permute-start.8 = (bf16[8,128,256]{2,1,0:T(8,128)(2,1)S(1)}, bf16[8,128,256]{2,1,0:T(8,128)(2,1)S(1)}, u32[]{:S(2)}, u32[]{:S(2)}) collective-permute-start(bf16[8,128,256]{2,1,0:T(8,128)(2,1)S(1)} %copy-done.13), channel_id=1, source_target_pairs={{16,0},{17,1},{18,2},{19,3},{20,4},{21,5},{22,6},{23,7},{24,8},{25... | collective-permute-start | bytes 1572872 | tf_op jit(solution)/shard_map/ppermute | solution.py:352
  143.8 10.3 %collective-permute-done.7.prev_ref = bf16[8,128,256]{2,1,0:T(8,128)(2,1)S(1)} collective-permute-done((bf16[8,128,256]{2,1,0:T(8,128)(2,1)S(1)}, bf16[8,128,256]{2,1,0:T(8,128)(2,1)S(1)}, u32[]{:S(2)}, u32[]{:S(2)}) %collective-permute-start.7) | collective-permute-done | bytes 524320 | tf_op jit(solution)/shard_map/ppermute | solution.py:352
  154.1 1.2 collective-permute-done.8.next_ref
  155.3 1.6 copy-done.4
  156.9 1.2 shard_map.49
  158.1 6.6 %all-to-all-start.3 = ((bf16[16,128,256]{2,1,0:T(8,128)(2,1)}), bf16[16,128,256]{2,1,0:T(8,128)(2,1)S(1)}, u32[]{:S(2)}, u32[]{:S(2)}) async-start(bf16[16,128,256]{2,1,0:T(8,128)(2,1)} %shard_map.49), calls=%async_computation.3 | async-start | bytes 2097152 | tf_op jit(solution)/shard_map/all_to_all | solution.py:356
  164.8 1.7 shard_map.52.held_ref
  166.5 14.8 %all-to-all-done.3.dkv_ref = bf16[16,128,256]{2,1,0:T(8,128)(2,1)S(1)} async-done(((bf16[16,128,256]{2,1,0:T(8,128)(2,1)}), bf16[16,128,256]{2,1,0:T(8,128)(2,1)S(1)}, u32[]{:S(2)}, u32[]{:S(2)}) %all-to-all-start.3) | async-done | bytes 1048608 | tf_op jit(solution)/shard_map/all_to_all | solution.py:356
  (65 shorter events, 11.9 us)
Async XLA Ops:
  0.0 1.9 %copy-start = (bf16[128,12288]{1,0:T(8,128)(2,1)S(1)}, bf16[128,12288]{1,0:T(8,128)(2,1)}, u32[]{:S(2)}) copy-start(bf16[128,12288]{1,0:T(8,128)(2,1)} %qkv_ref.3) | copy-start | bytes 9437188
  2.6 1.3 copy-start.2
  4.0 5.5 %copy-start.17 = (s32[4]{0:T(128)S(1)}, s32[4]{0:T(128)}, u32[]{:S(2)}) copy-start(s32[4]{0:T(128)} %param.7) | copy-start | bytes 52
  4.0 5.6 %copy-start.16 = (s32[4,4]{1,0:T(4,128)S(1)}, s32[4,4]{1,0:T(4,128)}, u32[]{:S(2)}) copy-start(s32[4,4]{1,0:T(4,128)} %param.6) | copy-start | bytes 196
  4.0 10.4 %copy-start.1 = (bf16[128,12288]{1,0:T(8,128)(2,1)S(1)}, bf16[128,12288]{1,0:T(8,128)(2,1)}, u32[]{:S(2)}) copy-start(bf16[128,12288]{1,0:T(8,128)(2,1)} %qkv_ref.3) | copy-start | bytes 9437188
  4.0 33.3 %all-to-all-start = ((bf16[16,2,128,256]{3,2,1,0:T(8,128)(2,1)}), bf16[16,2,128,256]{3,2,1,0:T(8,128)(2,1)}, u32[]{:S(2)}, u32[]{:S(2)}) async-start(bf16[16,2,128,256]{3,2,1,0:T(8,128)(2,1)} %copy-done.2), calls=%async_computation | async-start | bytes 4194304 | tf_op jit(solution)/shard_map/all_to_all | solution.py:340
  9.6 45.7 %collective-permute-start.2 = (s32[4,5]{1,0:T(4,128)S(1)}, s32[4,5]{1,0:T(4,128)S(1)}, u32[]{:S(2)}, u32[]{:S(2)}) collective-permute-start(s32[4,5]{1,0:T(4,128)S(1)} %pad_add_fusion.1), channel_id=1, source_target_pairs={{0,12},{4,0},{8,4},{12,8},{1,13},{5,1},{9,5},{13,9},{2,14},{6,2},{... | collective-permute-start | bytes 248 | tf_op jit(solution)/shard_map/ppermute | solution.py:328
  12.7 42.6 %collective-permute-start.1 = (s32[4,5]{1,0:T(4,128)S(1)}, s32[4,5]{1,0:T(4,128)S(1)}, u32[]{:S(2)}, u32[]{:S(2)}) collective-permute-start(s32[4,5]{1,0:T(4,128)S(1)} %pad_add_fusion.1), channel_id=1, source_target_pairs={{0,8},{4,12},{8,0},{12,4},{1,9},{5,13},{9,1},{13,5},{2,10},{6,14},... | collective-permute-start | bytes 248 | tf_op jit(solution)/shard_map/ppermute | solution.py:328
  13.6 41.8 %collective-permute-start = (s32[4,5]{1,0:T(4,128)S(1)}, s32[4,5]{1,0:T(4,128)S(1)}, u32[]{:S(2)}, u32[]{:S(2)}) collective-permute-start(s32[4,5]{1,0:T(4,128)S(1)} %pad_add_fusion.1), channel_id=1, source_target_pairs={{0,4},{4,8},{8,12},{12,0},{1,5},{5,9},{9,13},{13,1},{2,6},{6,10},{... | collective-permute-start | bytes 248 | tf_op jit(solution)/shard_map/ppermute | solution.py:328
  14.4 1.2 copy-start.5
  18.1 1.0 copy-start.6
  37.2 29.3 %all-to-all-start.1 = ((bf16[16,128,256]{2,1,0:T(8,128)(2,1)}), bf16[16,128,256]{2,1,0:T(8,128)(2,1)S(1)}, u32[]{:S(2)}, u32[]{:S(2)}) async-start(bf16[16,128,256]{2,1,0:T(8,128)(2,1)} %copy-done.6), calls=%async_computation.1 | async-start | bytes 2097152 | tf_op jit(solution)/shard_map/all_to_all | solution.py:344
  44.8 20.5 %collective-permute-start.3 = (bf16[8,128,256]{2,1,0:T(8,128)(2,1)S(1)}, bf16[8,128,256]{2,1,0:T(8,128)(2,1)S(1)}, u32[]{:S(2)}, u32[]{:S(2)}) collective-permute-start(bf16[8,128,256]{2,1,0:T(8,128)(2,1)S(1)} %get-tuple-element.44), channel_id=1, source_target_pairs={{0,16},{1,17},{2,18},{3,19},{4,20},{5,21},{6,22},{7,23},{8,24},{9,... | collective-permute-start | bytes 1572872 | tf_op jit(solution)/shard_map/ppermute | solution.py:342
  48.6 17.9 %collective-permute-start.4 = (bf16[8,128,256]{2,1,0:T(8,128)(2,1)S(1)}, bf16[8,128,256]{2,1,0:T(8,128)(2,1)S(1)}, u32[]{:S(2)}, u32[]{:S(2)}) collective-permute-start(bf16[8,128,256]{2,1,0:T(8,128)(2,1)S(1)} %get-tuple-element.43), channel_id=1, source_target_pairs={{16,0},{17,1},{18,2},{19,3},{20,4},{21,5},{22,6},{23,7},{24,8},{25... | collective-permute-start | bytes 1572872 | tf_op jit(solution)/shard_map/ppermute | solution.py:342
  65.3 9.2 %copy-start.8 = (bf16[8,128,256]{2,1,0:T(8,128)(2,1)}, bf16[8,128,256]{2,1,0:T(8,128)(2,1)S(1)}, u32[]{:S(2)}) copy-start(bf16[8,128,256]{2,1,0:T(8,128)(2,1)S(1)} %collective-permute-done.3.before_ref) | copy-start | bytes 1572868
  66.5 8.0 %copy-start.10 = (bf16[8,128,256]{2,1,0:T(8,128)(2,1)}, bf16[8,128,256]{2,1,0:T(8,128)(2,1)S(1)}, u32[]{:S(2)}) copy-start(bf16[8,128,256]{2,1,0:T(8,128)(2,1)S(1)} %collective-permute-done.4.after_ref) | copy-start | bytes 1572868
  66.5 38.6 %all-to-all-start.2 = ((bf16[16,128,256]{2,1,0:T(8,128)(2,1)}), bf16[16,128,256]{2,1,0:T(8,128)(2,1)}, u32[]{:S(2)}, u32[]{:S(2)}) async-start(bf16[16,128,256]{2,1,0:T(8,128)(2,1)} %get-tuple-element.29), calls=%async_computation.2 | async-start | bytes 2097152 | tf_op jit(solution)/shard_map/all_to_all | solution.py:347
  72.0 39.7 %collective-permute-start.5 = (bf16[8,128,256]{2,1,0:T(8,128)(2,1)}, bf16[8,128,256]{2,1,0:T(8,128)(2,1)}, u32[]{:S(2)}, u32[]{:S(2)}) collective-permute-start(bf16[8,128,256]{2,1,0:T(8,128)(2,1)} %get-tuple-element.27), channel_id=1, source_target_pairs={{0,16},{1,17},{2,18},{3,19},{4,20},{5,21},{6,22},{7,23},{8,24},{9,... | collective-permute-start | bytes 1572872 | tf_op jit(solution)/shard_map/ppermute | solution.py:346
  74.5 37.2 %collective-permute-start.6 = (bf16[8,128,256]{2,1,0:T(8,128)(2,1)}, bf16[8,128,256]{2,1,0:T(8,128)(2,1)}, u32[]{:S(2)}, u32[]{:S(2)}) collective-permute-start(bf16[8,128,256]{2,1,0:T(8,128)(2,1)} %get-tuple-element.28), channel_id=1, source_target_pairs={{16,0},{17,1},{18,2},{19,3},{20,4},{21,5},{22,6},{23,7},{24,8},{25... | collective-permute-start | bytes 1572872 | tf_op jit(solution)/shard_map/ppermute | solution.py:346
  81.5 1.0 copy-start.9
  82.5 1.0 copy-start.11
  97.1 30.1 %collective-permute-start.9 = (bf16[8,128,256]{2,1,0:T(8,128)(2,1)}, bf16[8,128,256]{2,1,0:T(8,128)(2,1)}, u32[]{:S(2)}, u32[]{:S(2)}) collective-permute-start(bf16[8,128,256]{2,1,0:T(8,128)(2,1)} %get-tuple-element.38), channel_id=1, source_target_pairs={{0,16},{1,17},{2,18},{3,19},{4,20},{5,21},{6,22},{7,23},{8,24},{9,... | collective-permute-start | bytes 1572872 | tf_op jit(solution)/shard_map/ppermute | solution.py:350
  99.1 28.2 %collective-permute-start.10 = (bf16[8,128,256]{2,1,0:T(8,128)(2,1)}, bf16[8,128,256]{2,1,0:T(8,128)(2,1)}, u32[]{:S(2)}, u32[]{:S(2)}) collective-permute-start(bf16[8,128,256]{2,1,0:T(8,128)(2,1)} %get-tuple-element.39), channel_id=1, source_target_pairs={{16,0},{17,1},{18,2},{19,3},{20,4},{21,5},{22,6},{23,7},{24,8},{25... | collective-permute-start | bytes 1572872 | tf_op jit(solution)/shard_map/ppermute | solution.py:350
  105.1 24.9 %all-to-all-start.4 = ((bf16[16,128,128]{2,1,0:T(8,128)(2,1)}), bf16[16,128,128]{2,1,0:T(8,128)(2,1)S(1)}, u32[]{:S(2)}, u32[]{:S(2)}) async-start(bf16[16,128,128]{2,1,0:T(8,128)(2,1)} %copy-done.7), calls=%async_computation.4 | async-start | bytes 1048576 | tf_op jit(solution)/shard_map/all_to_all | solution.py:353
  124.3 1.3 copy-start.3
  130.0 5.9 %copy-start.15 = (bf16[8,128,256]{2,1,0:T(8,128)(2,1)S(1)}, bf16[8,128,256]{2,1,0:T(8,128)(2,1)}, u32[]{:S(2)}) copy-start(bf16[8,128,256]{2,1,0:T(8,128)(2,1)} %copy-done.14) | copy-start | bytes 1572868
  130.0 7.8 %copy-start.13 = (bf16[8,128,256]{2,1,0:T(8,128)(2,1)S(1)}, bf16[8,128,256]{2,1,0:T(8,128)(2,1)}, u32[]{:S(2)}) copy-start(bf16[8,128,256]{2,1,0:T(8,128)(2,1)} %copy-done.12) | copy-start | bytes 1572868
  130.0 28.1 %all-to-all-start.5 = ((bf16[16,128,384]{2,1,0:T(8,128)(2,1)}), bf16[16,128,384]{2,1,0:T(8,128)(2,1)S(1)}, u32[]{:S(2)}, u32[]{:S(2)}) async-start(bf16[16,128,384]{2,1,0:T(8,128)(2,1)} %shard_map.51), calls=%async_computation.5 | async-start | bytes 3145728 | tf_op jit(solution)/shard_map/all_to_all | solution.py:354
  135.9 18.3 %collective-permute-start.7 = (bf16[8,128,256]{2,1,0:T(8,128)(2,1)S(1)}, bf16[8,128,256]{2,1,0:T(8,128)(2,1)S(1)}, u32[]{:S(2)}, u32[]{:S(2)}) collective-permute-start(bf16[8,128,256]{2,1,0:T(8,128)(2,1)S(1)} %copy-done.15), channel_id=1, source_target_pairs={{0,16},{1,17},{2,18},{3,19},{4,20},{5,21},{6,22},{7,23},{8,24},{9,... | collective-permute-start | bytes 1572872 | tf_op jit(solution)/shard_map/ppermute | solution.py:352
  137.8 17.5 %collective-permute-start.8 = (bf16[8,128,256]{2,1,0:T(8,128)(2,1)S(1)}, bf16[8,128,256]{2,1,0:T(8,128)(2,1)S(1)}, u32[]{:S(2)}, u32[]{:S(2)}) collective-permute-start(bf16[8,128,256]{2,1,0:T(8,128)(2,1)S(1)} %copy-done.13), channel_id=1, source_target_pairs={{16,0},{17,1},{18,2},{19,3},{20,4},{21,5},{22,6},{23,7},{24,8},{25... | collective-permute-start | bytes 1572872 | tf_op jit(solution)/shard_map/ppermute | solution.py:352
  155.3 1.6 copy-start.4
  158.1 23.1 %all-to-all-start.3 = ((bf16[16,128,256]{2,1,0:T(8,128)(2,1)}), bf16[16,128,256]{2,1,0:T(8,128)(2,1)S(1)}, u32[]{:S(2)}, u32[]{:S(2)}) async-start(bf16[16,128,256]{2,1,0:T(8,128)(2,1)} %shard_map.49), calls=%async_computation.3 | async-start | bytes 2097152 | tf_op jit(solution)/shard_map/all_to_all | solution.py:356
  (3 other events, 2.4 us)

commit v3 on v2

v3 whole, which is shorter than its diff:
```python
import functools

import jax
import jax.numpy as jnp
from jax import lax
from jax.experimental import pallas as pl
from jax.experimental.pallas import tpu as pltpu
from jax.sharding import Mesh
from jax.sharding import PartitionSpec as P

HD = 128
BLK = 128
TILES = 4
SPAN = 2
LISTED = 4
WIN = 3
RING = 4
GROUP = RING * TILES
HALO = SPAN * TILES
NAMED = 2
BACK = TILES + NAMED
EXT = GROUP + 2 * HALO
LOCAL = 2
SLOTS = WIN + LISTED
SIDES = 4
COLS = LOCAL * 3 * HD
LOG2E = 1.4426950408889634
F32 = jnp.float32
BF16 = jnp.bfloat16


VMEM = pl.BlockSpec(memory_space=pltpu.VMEM)
SMEM = pl.BlockSpec(memory_space=pltpu.SMEM)
HBM = pl.BlockSpec(memory_space=pl.ANY)


def run_all(pairs, sem):
    running = [pltpu.make_async_copy(s, d, sem.at[i]) for i, (s, d) in enumerate(pairs)]
    for c in running:
        c.start()
    for c in running:
        c.wait()


def columns(part, flip, head):
    pair = (part // 4) * 4 + jnp.bitwise_xor(part % 4, flip)
    at = pair * LOCAL + head
    return pl.multiple_of(at * 3 * HD, 3 * HD), pl.multiple_of(at * HD, HD)


def send_pairs_kernel(flip_ref, qkv_ref, kv_ref, sem):
    pairs = []
    for part in range(GROUP):
        for h in range(LOCAL):
            at, _ = columns(part, flip_ref[0], h)
            pairs.append((qkv_ref.at[:, pl.ds(at + HD, 2 * HD)], kv_ref.at[part, h]))
    run_all(pairs, sem)


def send_pairs(flip, qkv):
    return pl.pallas_call(
        send_pairs_kernel,
        out_shape=jax.ShapeDtypeStruct((GROUP, LOCAL, BLK, 2 * HD), BF16),
        in_specs=[SMEM, HBM],
        out_specs=VMEM,
        scratch_shapes=[pltpu.SemaphoreType.DMA((GROUP * LOCAL,))],
        compiler_params=pltpu.CompilerParams(vmem_limit_bytes=8 << 20),
        cost_estimate=pl.CostEstimate(flops=0, bytes_accessed=4 << 20, transcendentals=0),
    )(flip, qkv)


def send_queries_kernel(flip_ref, qkv_ref, grad_ref, qd_ref, sem):
    pairs = []
    for part in range(GROUP):
        for h in range(LOCAL):
            at, gat = columns(part, flip_ref[0], h)
            pairs.append((qkv_ref.at[:, pl.ds(at, HD)], qd_ref.at[part, h, :, pl.ds(0, HD)]))
            pairs.append((grad_ref.at[:, pl.ds(gat, HD)], qd_ref.at[part, h, :, pl.ds(HD, HD)]))
    run_all(pairs, sem)


def send_queries(flip, qkv, grad_out):
    return pl.pallas_call(
        send_queries_kernel,
        out_shape=jax.ShapeDtypeStruct((GROUP, LOCAL, BLK, 2 * HD), BF16),
        in_specs=[SMEM, HBM, HBM],
        out_specs=VMEM,
        scratch_shapes=[pltpu.SemaphoreType.DMA((GROUP * LOCAL * 2,))],
        compiler_params=pltpu.CompilerParams(vmem_limit_bytes=8 << 20),
        cost_estimate=pl.CostEstimate(flops=0, bytes_accessed=4 << 20, transcendentals=0),
    )(flip, qkv, grad_out)


def join_early_kernel(flip_ref, dq_ref, out_ref, sem):
    pairs = []
    for part in range(GROUP):
        for h in range(LOCAL):
            at, _ = columns(part, flip_ref[0], h)
            pairs.append((dq_ref.at[part, h], out_ref.at[:, pl.ds(at, HD)]))
    run_all(pairs, sem)


def join_early(flip, dq):
    return pl.pallas_call(
        join_early_kernel,
        out_shape=jax.ShapeDtypeStruct((BLK, GROUP * COLS), BF16),
        in_specs=[SMEM, VMEM],
        out_specs=HBM,
        scratch_shapes=[pltpu.SemaphoreType.DMA((GROUP * LOCAL,))],
        compiler_params=pltpu.CompilerParams(vmem_limit_bytes=8 << 20),
        cost_estimate=pl.CostEstimate(flops=0, bytes_accessed=2 << 20, transcendentals=0),
    )(flip, dq)


def join_late_kernel(flip_ref, dkv_ref, held_ref, out_ref, sem):
    pairs = []
    for part in range(GROUP):
        for h in range(LOCAL):
            at, _ = columns(part, flip_ref[0], h)
            pairs.append((dkv_ref.at[part, h], out_ref.at[:, pl.ds(at + HD, 2 * HD)]))
    run_all(pairs, sem)


def join_late(flip, dkv, held):
    return pl.pallas_call(
        join_late_kernel,
        out_shape=jax.ShapeDtypeStruct((BLK, GROUP * COLS), BF16),
        in_specs=[SMEM, VMEM, HBM],
        out_specs=HBM,
        scratch_shapes=[pltpu.SemaphoreType.DMA((GROUP * LOCAL,))],
        input_output_aliases={2: 0},
        compiler_params=pltpu.CompilerParams(vmem_limit_bytes=8 << 20),
        cost_estimate=pl.CostEstimate(flops=0, bytes_accessed=4 << 20, transcendentals=0),
    )(flip, dkv, held)


def add_kernel(ask_ref, own_ref, prev_ref, next_ref, out_ref):
    zero = jnp.zeros((), F32)
    for b in range(GROUP):
        for h in range(LOCAL):
            total = own_ref[b, h].astype(F32)
            if b < TILES:
                total = total + prev_ref[b, h].astype(F32)
            elif b < 2 * TILES:
                for i in range(NAMED):
                    hit = ask_ref[1, i] == b - TILES
                    total = total + jnp.where(hit, prev_ref[TILES + i, h].astype(F32), zero)
            elif b < GROUP - TILES:
                for i in range(NAMED):
                    hit = ask_ref[0, i] == b - (GROUP - 2 * TILES)
                    total = total + jnp.where(hit, next_ref[i, h].astype(F32), zero)
            else:
                total = total + next_ref[NAMED + b - (GROUP - TILES), h].astype(F32)
            out_ref[b, h] = total.astype(BF16)


def add_halo(ask, own, from_prev, from_next):
    return pl.pallas_call(
        add_kernel,
        out_shape=jax.ShapeDtypeStruct((GROUP, LOCAL, BLK, 2 * HD), BF16),
        in_specs=[SMEM] + [VMEM] * 3,
        out_specs=VMEM,
        compiler_params=pltpu.CompilerParams(vmem_limit_bytes=12 << 20),
        cost_estimate=pl.CostEstimate(flops=4 << 20, bytes_accessed=8 << 20, transcendentals=0),
    )(ask, own, from_prev, from_next)


def attention_kernel(
    place_ref,
    live_ref,
    want_ref,
    kv_ref,
    before_ref,
    after_ref,
    qd_ref,
    dq_ref,
    own_ref,
    tobefore_ref,
    toafter_ref,
    kv,
    qd,
    acc,
    mix,
    chosen,
    tall,
    low,
    dqs,
    outs,
    came,
    left,
):
    loads, stores = [], []
    for h in range(LOCAL):
        here = [
            (before_ref.at[:, h], kv.at[h, pl.ds(0, HALO)]),
            (kv_ref.at[:, h], kv.at[h, pl.ds(HALO, GROUP)]),
            (after_ref.at[:, h], kv.at[h, pl.ds(HALO + GROUP, HALO)]),
            (qd_ref.at[:, h], qd.at[h]),
        ]
        there = [
            (dqs.at[h], dq_ref.at[:, h]),
            (outs.at[h, pl.ds(TILES, TILES)], tobefore_ref.at[pl.ds(NAMED, TILES), h]),
            (outs.at[h, pl.ds(HALO, TILES)], toafter_ref.at[pl.ds(0, TILES), h]),
        ]
        for i in range(NAMED):
            there.append((outs.at[h, want_ref[0, i]], tobefore_ref.at[i, h]))
            there.append(
                (outs.at[h, HALO + TILES + want_ref[1, i]], toafter_ref.at[TILES + i, h])
            )
        loads.append([pltpu.make_async_copy(s, d, came.at[h, i]) for i, (s, d) in enumerate(here)])
        stores.append([pltpu.make_async_copy(s, d, left.at[h, i]) for i, (s, d) in enumerate(there)])
    for h in range(LOCAL):
        for c in loads[h]:
            c.start()
    acc[...] = jnp.zeros_like(acc)
    mix[...] = jnp.zeros_like(mix)
    for c in loads[0]:
        c.wait()
    scale = HD ** (-0.5)
    column = lax.broadcasted_iota(jnp.int32, (1, 1, 2 * HD), 2)
    factor = jnp.where(column < HD, scale, 1.0).astype(F32)

    def begin(head, block, side):
        mix[side, 0:BLK, 0:HD] = qd[head, block, :, 0:HD]
        mix[side, BLK : 2 * BLK, HD : 2 * HD] = qd[head, block, :, HD : 2 * HD]
        for j in range(SLOTS):
            chosen[side, j * BLK : (j + 1) * BLK] = kv[head, place_ref[block, j]]
        tall[side] = lax.dot_general(
            chosen[side], mix[side], (((1,), (1,)), ((), ())), preferred_element_type=F32
        )

    def middle(block, side):
        high = jnp.full((8, BLK), -3e38, F32)
        biases = [jnp.where(live_ref[block, j] > 0, 0.0, -1e30).astype(F32) for j in range(SLOTS)]
        for j in range(SLOTS):
            scores = tall[side, j * BLK : (j + 1) * BLK, 0:BLK] * (scale * LOG2E) + biases[j]
            high = jnp.maximum(high, jnp.max(scores.reshape(BLK // 8, 8, BLK), axis=0))
        top = jnp.max(high, axis=0, keepdims=True)
        total = jnp.zeros((8, BLK), F32)
        cross = jnp.zeros((8, BLK), F32)
        for j in range(SLOTS):
            rows = slice(j * BLK, (j + 1) * BLK)
            powers = jnp.exp2(tall[side, rows, 0:BLK] * (scale * LOG2E) + (biases[j] - top))
            tall[side, rows, 0:BLK] = powers
            total = total + jnp.sum(powers.reshape(BLK // 8, 8, BLK), axis=0)
            cross = cross + jnp.sum(
                (powers * tall[side, rows, BLK : 2 * BLK]).reshape(BLK // 8, 8, BLK), axis=0
            )
        inverse = 1.0 / jnp.sum(total, axis=0, keepdims=True)
        delta = jnp.sum(cross, axis=0, keepdims=True) * inverse
        for j in range(SLOTS):
            rows = slice(j * BLK, (j + 1) * BLK)
            soft = tall[side, rows, 0:BLK] * inverse
            low[side, rows, 0:BLK] = (soft * (tall[side, rows, BLK : 2 * BLK] - delta)).astype(BF16)
            low[side, rows, BLK : 2 * BLK] = soft.astype(BF16)

    def end(head, block, side):
        grad_query = lax.dot_general(
            low[side, :, 0:BLK],
            chosen[side, :, 0:HD],
            (((0,), (0,)), ((), ())),
            preferred_element_type=F32,
        )
        dqs[head, block] = (grad_query * scale).astype(BF16)
        back = lax.dot_general(
            low[side], mix[side], (((1,), (0,)), ((), ())), preferred_element_type=F32
        )
        for j in range(SLOTS):
            acc[head, place_ref[block, j]] += back[j * BLK : (j + 1) * BLK]

    def step(head):
        def run(i, _):
            for k in range(SIDES):
                begin(head, SIDES * i + k, k)
            for k in range(SIDES):
                middle(SIDES * i + k, k)
            for k in range(SIDES):
                end(head, SIDES * i + k, k)
            return 0

        return run

    for h in range(LOCAL):
        if h > 0:
            for c in loads[h]:
                c.wait()
        lax.fori_loop(0, GROUP // SIDES, step(h), 0)
        outs[h, 0:HALO] = (acc[h, 0:HALO] * factor).astype(BF16)
        outs[h, HALO:] = (acc[h, HALO + GROUP :] * factor).astype(BF16)
        for c in stores[h]:
            c.start()
        own_ref[:, h] = (acc[h, HALO : HALO + GROUP] * factor).astype(BF16)
    for h in range(LOCAL):
        for c in stores[h]:
            c.wait()


def attention(places, live, wants, kv, before, after, qd):
    return pl.pallas_call(
        attention_kernel,
        out_shape=[
            pltpu.HBM((GROUP, LOCAL, BLK, HD), BF16),
            jax.ShapeDtypeStruct((GROUP, LOCAL, BLK, 2 * HD), BF16),
            pltpu.HBM((BACK, LOCAL, BLK, 2 * HD), BF16),
            pltpu.HBM((BACK, LOCAL, BLK, 2 * HD), BF16),
        ],
        in_specs=[SMEM, SMEM, SMEM, HBM, HBM, HBM, HBM],
        out_specs=[HBM, VMEM, HBM, HBM],
        scratch_shapes=[
            pltpu.VMEM((LOCAL, EXT, BLK, 2 * HD), BF16),
            pltpu.VMEM((LOCAL, GROUP, BLK, 2 * HD), BF16),
            pltpu.VMEM((LOCAL, EXT, BLK, 2 * HD), F32),
            pltpu.VMEM((SIDES, 2 * BLK, 2 * HD), BF16),
            pltpu.VMEM((SIDES, SLOTS * BLK, 2 * HD), BF16),
            pltpu.VMEM((SIDES, SLOTS * BLK, 2 * BLK), F32),
            pltpu.VMEM((SIDES, SLOTS * BLK, 2 * BLK), BF16),
            pltpu.VMEM((LOCAL, GROUP, BLK, HD), BF16),
            pltpu.VMEM((LOCAL, 2 * HALO, BLK, 2 * HD), BF16),
            pltpu.SemaphoreType.DMA((LOCAL, 4)),
            pltpu.SemaphoreType.DMA((LOCAL, 3 + 2 * NAMED)),
        ],
        compiler_params=pltpu.CompilerParams(vmem_limit_bytes=30 << 20),
        cost_estimate=pl.CostEstimate(
            flops=4_800_000_000, bytes_accessed=16 << 20, transcendentals=4_000_000
        ),
    )(places, live, wants, *(pltpu.with_memory_space_constraint(x, pltpu.HBM) for x in (kv, before, after, qd)))


def shards(qkv, grad_out, key_lists, live_counts):
    planes = lax.axis_size("zz")
    plane = lax.axis_index("zz")
    team = ("x", "head")
    half = planes // 2
    flip = jnp.where(plane >= half, 2, 0).astype(jnp.int32).reshape(1)

    def crossing(step):
        pairs = []
        for p in range(planes):
            q = p + step
            if 0 <= q < planes:
                for r in range(RING):
                    for h in range(4):
                        other = h ^ 2 if (p >= half) != (q >= half) else h
                        pairs.append(((p * RING + r) * 4 + h, (q * RING + r) * 4 + other))
        return pairs

    everyone = ("zz", "x", "head")
    to_next = functools.partial(lax.ppermute, axis_name=everyone, perm=crossing(1))
    to_prev = functools.partial(lax.ppermute, axis_name=everyone, perm=crossing(-1))

    named = jnp.concatenate([key_lists, live_counts[:, None]], axis=1)
    ring = [named]
    for step in range(1, RING):
        ring.append(lax.ppermute(named, "x", [(i, (i + step) % RING) for i in range(RING)]))
    behind = jnp.mod(lax.axis_index("x") - jnp.arange(RING, dtype=jnp.int32), RING)
    named = jnp.take(jnp.stack(ring), behind, axis=0).reshape(GROUP, LISTED + 1)
    blocks = plane * GROUP + jnp.arange(GROUP, dtype=jnp.int32)
    window = blocks[:, None] - 1 + jnp.arange(WIN, dtype=jnp.int32)[None, :]
    window_ok = (window >= 0) & (window < planes * GROUP)
    listed_ok = jnp.arange(LISTED, dtype=jnp.int32)[None, :] < named[:, LISTED:]
    live = jnp.concatenate([window_ok, listed_ok], axis=1).astype(jnp.int32)
    places = jnp.concatenate([window, named[:, :LISTED]], axis=1) - plane * GROUP + HALO

    order = jnp.arange(TILES, dtype=jnp.int32)
    ends = jnp.stack([order, order + EXT - TILES])
    needed = jnp.any(places[None, :, :, None] == ends[:, None, None, :], axis=(1, 2))
    wants = jnp.stack(
        [
            jnp.min(jnp.where(needed, order, TILES - 1), axis=1),
            jnp.max(jnp.where(needed, order, 0), axis=1),
        ],
        axis=1,
    ).astype(jnp.int32)
    ask = jnp.stack([to_prev(wants[0]), to_next(wants[1])])
    once = jnp.where(ask[:, 1] == ask[:, 0], -1, ask[:, 1])
    ask = jnp.stack([ask[:, 0], once], axis=1)

    swap = functools.partial(lax.all_to_all, axis_name=team, split_axis=0, concat_axis=0, tiled=True)
    qd = send_queries(flip, qkv, grad_out)
    kv = swap(send_pairs(flip, qkv))
    kv, qd = lax.optimization_barrier((kv, qd))
    qd, ask = lax.optimization_barrier((swap(qd), ask))
    before, after = to_next(kv[GROUP - HALO :]), to_prev(kv[:HALO])
    dq, own, tobefore, toafter = attention(places, live, wants, kv, before, after, qd)
    from_prev, from_next = to_next(toafter), to_prev(tobefore)
    held = join_early(flip, swap(dq))
    dkv = swap(add_halo(ask, own, from_prev, from_next))
    return join_late(flip, dkv, held)


def solution(mesh):
    shape = mesh.devices.shape
    inner = Mesh(mesh.devices.reshape(shape[0] // RING, RING, shape[1]), ("zz", "x", "head"))
    everyone = ("zz", "x", "head")
    placed = (P(everyone, None), P(everyone, None), P(("zz", "x"), None), P(("zz", "x")))
    return jax.shard_map(
        shards, mesh=inner, in_specs=placed, out_specs=P(everyone, None), check_vma=False
    )
```

time: 183 us -> 182 us (level)
  waiting for transfers between devices: 54.8 us -> 81.1 us
  starting transfers between devices: 74.7 us -> 54.6 us
  local copies, waits for them, and re-layouts: 16.6 us -> 11.5 us
  Pallas kernels: 35.3 us -> 31.3 us
    ppermute x3, waiting for transfers between devices: 0.01 us -> 18.1 us  [shards(): lax.ppermute(named, 'x', [(i, (i + step) % RING) for i in range(RING)])]
    all_to_all x1, waiting for transfers between devices: 18 us -> 0.01 us  [shards(): kv = swap(send_pairs(flip, qkv))]
    ppermute x8 -> x6, waiting for transfers between devices: 22 us -> 36.4 us  [the longest x2 19 us: shards(): ask = jnp.stack([to_prev(wants[0]), to_next(wants[1])])]
    all_to_all x5 -> x3, starting transfers between devices: 29 us -> 16.6 us  [the longest x1 6.63 us: shards(): dkv = swap(add_halo(ask, own, from_prev, from_next))]
    all_to_all x5 -> x3, waiting for transfers between devices: 14.8 us -> 26.5 us  [the longest x1 26.5 us: shards(): dkv = swap(add_halo(ask, own, from_prev, from_next))]
    ppermute x8 -> x6, starting transfers between devices: 35.5 us -> 26 us  [the longest x2 10.1 us: shards(): before, after = (to_next(kv[GROUP - HALO:]), to_prev(kv[:HALO]))]
    unnamed x36 -> x16, local copies, waits for them, and re-layouts: 12.8 us -> 7.07 us
    pallas_call x5 -> x3, Pallas kernels: 31.7 us -> 27.8 us  [the longest x1 23.7 us: attention(): pl.pallas_call(attention_kernel, out_shape=[pltpu.HBM((GROUP, LOCAL, BLK,...]
  transfers between devices with their start and end apart: 17 -> 13, of which waited for: 6 -> 6; matrix products, arithmetic and copies ran while one was open for 2% -> 3% of each run, Pallas kernels for 18% -> 3%
where the time goes in v3:
time: 182 us; the launch traced here: 180 us
  waiting for transfers between devices  81.1 us (45%)
  starting transfers between devices  54.6 us (30%)
  Pallas kernels  31.3 us (17%)
  local copies, waits for them, and re-layouts  11.5 us (6%)
    all_to_all x1, waiting for transfers between devices, shards(): dkv = swap(add_halo(ask, own, from_prev, from_next))  26.5 us
    pallas_call x1, Pallas kernels, attention(): pl.pallas_call(attention_kernel, out_shape=[pltpu.HBM((GROUP, LOCAL, BLK,...  23.7 us
    ppermute x2, waiting for transfers between devices, shards(): ask = jnp.stack([to_prev(wants[0]), to_next(wants[1])])  19 us
    ppermute x3, waiting for transfers between devices, shards(): lax.ppermute(named, 'x', [(i, (i + step) % RING) for i in range(RING)])  18.1 us
    ppermute x2, waiting for transfers between devices, shards(): from_prev, from_next = (to_next(toafter), to_prev(tobefore))  17.4 us
    ppermute x2, starting transfers between devices, shards(): before, after = (to_next(kv[GROUP - HALO:]), to_prev(kv[:HALO]))  10.1 us
    ppermute x2, starting transfers between devices, shards(): ask = jnp.stack([to_prev(wants[0]), to_next(wants[1])])  7.95 us
    ppermute x2, starting transfers between devices, shards(): from_prev, from_next = (to_next(toafter), to_prev(tobefore))  7.95 us
  transfers between devices with their start and end apart: 13, of which 6 were waited for; matrix products, arithmetic and copies ran while one was open for 3% of the time, Pallas kernels for 3%

profile of v3, /device:TPU:16, one launch (start us, length us, event | category | flops | bytes accessed | tf_op | source)
XLA Modules:
  0.0 180.0 jit_solution(17332646981534438835)
XLA Ops:
  0.0 1.9 %copy-done = bf16[128,12288]{1,0:T(8,128)(2,1)S(1)} copy-done((bf16[128,12288]{1,0:T(8,128)(2,1)S(1)}, bf16[128,12288]{1,0:T(8,128)(2,1)}, u32[]{:S(2)}) %copy-start) | copy-done | bytes 3145752
  1.9 0.7 shard_map.46
  2.7 1.3 copy-done.3
  4.0 5.4 %all-to-all-start = ((bf16[16,2,128,256]{3,2,1,0:T(8,128)(2,1)}), bf16[16,2,128,256]{3,2,1,0:T(8,128)(2,1)}, u32[]{:S(2)}, u32[]{:S(2)}) async-start(bf16[16,2,128,256]{3,2,1,0:T(8,128)(2,1)} %copy-done.3), calls=%async_computation | async-start | bytes 4194304 | tf_op jit(solution)/shard_map/all_to_all | solution.py:380
  9.6 3.4 %collective-permute-start.1 = (s32[4,5]{1,0:T(4,128)S(1)}, s32[4,5]{1,0:T(4,128)S(1)}, u32[]{:S(2)}, u32[]{:S(2)}) collective-permute-start(s32[4,5]{1,0:T(4,128)S(1)} %pad_add_fusion.1), channel_id=1, source_target_pairs={{0,8},{4,12},{8,0},{12,4},{1,9},{5,13},{9,1},{13,5},{2,10},{6,14},... | collective-permute-start | bytes 248 | tf_op jit(solution)/shard_map/ppermute | solution.py:354
  13.0 0.6 collective-permute-start
  13.6 2.7 %collective-permute-start.2 = (s32[4,5]{1,0:T(4,128)S(1)}, s32[4,5]{1,0:T(4,128)S(1)}, u32[]{:S(2)}, u32[]{:S(2)}) collective-permute-start(s32[4,5]{1,0:T(4,128)S(1)} %pad_add_fusion.1), channel_id=1, source_target_pairs={{0,12},{4,0},{8,4},{12,8},{1,13},{5,1},{9,5},{13,9},{2,14},{6,2},{... | collective-permute-start | bytes 248 | tf_op jit(solution)/shard_map/ppermute | solution.py:354
  16.7 1.2 copy-done.4
  17.9 1.5 shard_map.47
  19.4 1.3 copy-done.2
  20.7 18.1 %collective-permute-done.1 = s32[4,5]{1,0:T(4,128)S(1)} collective-permute-done((s32[4,5]{1,0:T(4,128)S(1)}, s32[4,5]{1,0:T(4,128)S(1)}, u32[]{:S(2)}, u32[]{:S(2)}) %collective-permute-start.1) | collective-permute-done | bytes 112 | tf_op jit(solution)/shard_map/ppermute | solution.py:354
  38.9 0.6 gather_fusion
  39.4 3.7 %all-to-all-start.1 = ((bf16[16,2,128,256]{3,2,1,0:T(8,128)(2,1)}), bf16[16,2,128,256]{3,2,1,0:T(8,128)(2,1)S(1)}, u32[]{:S(2)}, u32[]{:S(2)}) async-start(bf16[16,2,128,256]{3,2,1,0:T(8,128)(2,1)} %copy-done.2), calls=%async_computation.1 | async-start | bytes 4194304 | tf_op jit(solution)/shard_map/all_to_all | solution.py:382
  44.1 3.1 %fusion.4 = (bf16[8,2,128,256]{3,2,1,0:T(8,128)(2,1)}, bf16[8,2,128,256]{3,2,1,0:T(8,128)(2,1)}) fusion(bf16[16,2,128,256]{3,2,1,0:T(8,128)(2,1)} %all-to-all-done.kv_ref), kind=kLoop, calls=%fused_computation.36 | loop fusion | bytes 4194304 | tf_op jit(solution)/shard_map/slice | solution.py:383
  47.2 8.2 %collective-permute-start.6 = (bf16[8,2,128,256]{3,2,1,0:T(8,128)(2,1)}, bf16[8,2,128,256]{3,2,1,0:T(8,128)(2,1)}, u32[]{:S(2)}, u32[]{:S(2)}) collective-permute-start(bf16[8,2,128,256]{3,2,1,0:T(8,128)(2,1)} %get-tuple-element.23), channel_id=1, source_target_pairs={{16,0},{17,1},{18,2},{19,3},{20,4},{21,5},{22,6},{23,7},{24,8},{25... | collective-permute-start | bytes 3145736 | tf_op jit(solution)/shard_map/ppermute | solution.py:383
  55.4 1.9 %collective-permute-start.5 = (bf16[8,2,128,256]{3,2,1,0:T(8,128)(2,1)}, bf16[8,2,128,256]{3,2,1,0:T(8,128)(2,1)}, u32[]{:S(2)}, u32[]{:S(2)}) collective-permute-start(bf16[8,2,128,256]{3,2,1,0:T(8,128)(2,1)} %get-tuple-element.24), channel_id=1, source_target_pairs={{0,16},{1,17},{2,18},{3,19},{4,20},{5,21},{6,22},{7,23},{8,24},{9,... | collective-permute-start | bytes 3145736 | tf_op jit(solution)/shard_map/ppermute | solution.py:383
  57.3 6.0 %collective-permute-start.3 = (s32[2]{0:T(128)S(1)}, s32[2]{0:T(128)S(1)}, u32[]{:S(2)}, u32[]{:S(2)}) collective-permute-start(s32[2]{0:T(128)S(1)} %get-tuple-element.27), channel_id=1, source_target_pairs={{16,0},{17,1},{18,2},{19,3},{20,4},{21,5},{22,6},{23,7},{24,8},{25... | collective-permute-start | bytes 32 | tf_op jit(solution)/shard_map/ppermute | solution.py:374
  63.4 1.9 %collective-permute-start.4 = (s32[2]{0:T(128)S(1)}, s32[2]{0:T(128)S(1)}, u32[]{:S(2)}, u32[]{:S(2)}) collective-permute-start(s32[2]{0:T(128)S(1)} %get-tuple-element.28), channel_id=1, source_target_pairs={{0,16},{1,17},{2,18},{3,19},{4,20},{5,21},{6,22},{7,23},{8,24},{9,... | collective-permute-start | bytes 32 | tf_op jit(solution)/shard_map/ppermute | solution.py:374
  65.6 12.8 %collective-permute-done.3 = s32[2]{0:T(128)S(1)} collective-permute-done((s32[2]{0:T(128)S(1)}, s32[2]{0:T(128)S(1)}, u32[]{:S(2)}, u32[]{:S(2)}) %collective-permute-start.3) | collective-permute-done | bytes 40 | tf_op jit(solution)/shard_map/ppermute | solution.py:374
  78.4 6.2 %collective-permute-done.4 = s32[2]{0:T(128)S(1)} collective-permute-done((s32[2]{0:T(128)S(1)}, s32[2]{0:T(128)S(1)}, u32[]{:S(2)}, u32[]{:S(2)}) %collective-permute-start.4) | collective-permute-done | bytes 40 | tf_op jit(solution)/shard_map/ppermute | solution.py:374
  84.8 1.3 copy-done.5
  86.1 23.7 %shard_map.48 = (bf16[16,2,128,128]{3,2,1,0:T(8,128)(2,1)}, bf16[16,2,128,256]{3,2,1,0:T(8,128)(2,1)S(1)}, bf16[6,2,128,256]{3,2,1,0:T(8,128)(2,1)}, bf16[6,2,128,256]{3,2,1,0:T(8,128)(2,1)}) custom-call(s32[16,7]{1,0:T(8,128)S(1)} %fusion.place_ref, s32[16,7]{1,0:T(8,128)S(1)} %add_convert_fusion.live_ref, s32[2,2]{1,0:T(2,128)S(1)} %pad_add_fusion.3.want_ref, ...), custom_call_target="tpu_custom_call" | custom-call | flops 4800000000 | bytes 16777216 | tf_op jit(solution)/shard_map/pallas_call | solution.py:299
  109.8 6.2 %all-to-all-start.3 = ((bf16[16,2,128,128]{3,2,1,0:T(8,128)(2,1)}), bf16[16,2,128,128]{3,2,1,0:T(8,128)(2,1)S(1)}, u32[]{:S(2)}, u32[]{:S(2)}) async-start(bf16[16,2,128,128]{3,2,1,0:T(8,128)(2,1)} %get-tuple-element.20), calls=%async_computation.3 | async-start | bytes 2097152 | tf_op jit(solution)/shard_map/all_to_all | solution.py:386
  116.0 1.9 %collective-permute-start.7 = (bf16[6,2,128,256]{3,2,1,0:T(8,128)(2,1)}, bf16[6,2,128,256]{3,2,1,0:T(8,128)(2,1)S(1)}, u32[]{:S(2)}, u32[]{:S(2)}) collective-permute-start(bf16[6,2,128,256]{3,2,1,0:T(8,128)(2,1)} %get-tuple-element.18), channel_id=1, source_target_pairs={{0,16},{1,17},{2,18},{3,19},{4,20},{5,21},{6,22},{7,23},{8,24},{9,... | collective-permute-start | bytes 2359304 | tf_op jit(solution)/shard_map/ppermute | solution.py:385
  118.0 6.0 %collective-permute-start.8 = (bf16[6,2,128,256]{3,2,1,0:T(8,128)(2,1)}, bf16[6,2,128,256]{3,2,1,0:T(8,128)(2,1)S(1)}, u32[]{:S(2)}, u32[]{:S(2)}) collective-permute-start(bf16[6,2,128,256]{3,2,1,0:T(8,128)(2,1)} %get-tuple-element.19), channel_id=1, source_target_pairs={{16,0},{17,1},{18,2},{19,3},{20,4},{21,5},{22,6},{23,7},{24,8},{25... | collective-permute-start | bytes 2359304 | tf_op jit(solution)/shard_map/ppermute | solution.py:385
  124.0 16.1 %collective-permute-done.7.prev_ref = bf16[6,2,128,256]{3,2,1,0:T(8,128)(2,1)S(1)} collective-permute-done((bf16[6,2,128,256]{3,2,1,0:T(8,128)(2,1)}, bf16[6,2,128,256]{3,2,1,0:T(8,128)(2,1)S(1)}, u32[]{:S(2)}, u32[]{:S(2)}) %collective-permute-start.7) | collective-permute-done | bytes 786464 | tf_op jit(solution)/shard_map/ppermute | solution.py:385
  140.1 1.3 collective-permute-done.8.next_ref
  141.4 2.6 %shard_map.49 = bf16[16,2,128,256]{3,2,1,0:T(8,128)(2,1)} custom-call(s32[2,2]{1,0:T(2,128)S(1)} %pad_add_fusion.5.ask_ref, bf16[16,2,128,256]{3,2,1,0:T(8,128)(2,1)S(1)} %get-tuple-element.17.own_ref, bf16[6,2,128,256]{3,2,1,0:T(8,128)(2,1)S(1)} %collective-permute-done.7.prev_ref, bf16[6,2,128,256]{3,2,1,0:T(8,128)(2,1)S(1)} %collective-permute-done.8.next_ref), custom_call_target="tpu_custom_call" | custom-call | flops 4194304 | bytes 8388608 | tf_op jit(solution)/shard_map/pallas_call | solution.py:158
  144.0 6.6 %all-to-all-start.2 = ((bf16[16,2,128,256]{3,2,1,0:T(8,128)(2,1)}), bf16[16,2,128,256]{3,2,1,0:T(8,128)(2,1)S(1)}, u32[]{:S(2)}, u32[]{:S(2)}) async-start(bf16[16,2,128,256]{3,2,1,0:T(8,128)(2,1)} %shard_map.49), calls=%async_computation.2 | async-start | bytes 4194304 | tf_op jit(solution)/shard_map/all_to_all | solution.py:387
  150.7 1.2 shard_map.50.held_ref
  151.9 26.5 %all-to-all-done.2.dkv_ref = bf16[16,2,128,256]{3,2,1,0:T(8,128)(2,1)S(1)} async-done(((bf16[16,2,128,256]{3,2,1,0:T(8,128)(2,1)}), bf16[16,2,128,256]{3,2,1,0:T(8,128)(2,1)S(1)}, u32[]{:S(2)}, u32[]{:S(2)}) %all-to-all-start.2) | async-done | bytes 2097184 | tf_op jit(solution)/shard_map/all_to_all | solution.py:387
  178.4 1.6 shard_map.51
  (48 shorter events, 2.0 us)
Async XLA Ops:
  0.0 1.9 %copy-start = (bf16[128,12288]{1,0:T(8,128)(2,1)S(1)}, bf16[128,12288]{1,0:T(8,128)(2,1)}, u32[]{:S(2)}) copy-start(bf16[128,12288]{1,0:T(8,128)(2,1)} %qkv_ref.3) | copy-start | bytes 9437188
  2.6 1.3 copy-start.3
  4.0 5.5 %copy-start.7 = (s32[4]{0:T(128)S(1)}, s32[4]{0:T(128)}, u32[]{:S(2)}) copy-start(s32[4]{0:T(128)} %param.7) | copy-start | bytes 52
  4.0 5.6 %copy-start.6 = (s32[4,4]{1,0:T(4,128)S(1)}, s32[4,4]{1,0:T(4,128)}, u32[]{:S(2)}) copy-start(s32[4,4]{1,0:T(4,128)} %param.6) | copy-start | bytes 196
  4.0 12.7 %copy-start.1 = (bf16[128,12288]{1,0:T(8,128)(2,1)S(1)}, bf16[128,12288]{1,0:T(8,128)(2,1)}, u32[]{:S(2)}) copy-start(bf16[128,12288]{1,0:T(8,128)(2,1)} %qkv_ref.3) | copy-start | bytes 9437188
  4.0 35.5 %all-to-all-start = ((bf16[16,2,128,256]{3,2,1,0:T(8,128)(2,1)}), bf16[16,2,128,256]{3,2,1,0:T(8,128)(2,1)}, u32[]{:S(2)}, u32[]{:S(2)}) async-start(bf16[16,2,128,256]{3,2,1,0:T(8,128)(2,1)} %copy-done.3), calls=%async_computation | async-start | bytes 4194304 | tf_op jit(solution)/shard_map/all_to_all | solution.py:380
  9.6 29.2 %collective-permute-start.1 = (s32[4,5]{1,0:T(4,128)S(1)}, s32[4,5]{1,0:T(4,128)S(1)}, u32[]{:S(2)}, u32[]{:S(2)}) collective-permute-start(s32[4,5]{1,0:T(4,128)S(1)} %pad_add_fusion.1), channel_id=1, source_target_pairs={{0,8},{4,12},{8,0},{12,4},{1,9},{5,13},{9,1},{13,5},{2,10},{6,14},... | collective-permute-start | bytes 248 | tf_op jit(solution)/shard_map/ppermute | solution.py:354
  13.0 25.9 %collective-permute-start = (s32[4,5]{1,0:T(4,128)S(1)}, s32[4,5]{1,0:T(4,128)S(1)}, u32[]{:S(2)}, u32[]{:S(2)}) collective-permute-start(s32[4,5]{1,0:T(4,128)S(1)} %pad_add_fusion.1), channel_id=1, source_target_pairs={{0,4},{4,8},{8,12},{12,0},{1,5},{5,9},{9,13},{13,1},{2,6},{6,10},{... | collective-permute-start | bytes 248 | tf_op jit(solution)/shard_map/ppermute | solution.py:354
  13.6 25.3 %collective-permute-start.2 = (s32[4,5]{1,0:T(4,128)S(1)}, s32[4,5]{1,0:T(4,128)S(1)}, u32[]{:S(2)}, u32[]{:S(2)}) collective-permute-start(s32[4,5]{1,0:T(4,128)S(1)} %pad_add_fusion.1), channel_id=1, source_target_pairs={{0,12},{4,0},{8,4},{12,8},{1,13},{5,1},{9,5},{13,9},{2,14},{6,2},{... | collective-permute-start | bytes 248 | tf_op jit(solution)/shard_map/ppermute | solution.py:354
  16.7 1.2 copy-start.4
  19.4 1.3 copy-start.2
  39.4 45.4 %all-to-all-start.1 = ((bf16[16,2,128,256]{3,2,1,0:T(8,128)(2,1)}), bf16[16,2,128,256]{3,2,1,0:T(8,128)(2,1)S(1)}, u32[]{:S(2)}, u32[]{:S(2)}) async-start(bf16[16,2,128,256]{3,2,1,0:T(8,128)(2,1)} %copy-done.2), calls=%async_computation.1 | async-start | bytes 4194304 | tf_op jit(solution)/shard_map/all_to_all | solution.py:382
  47.2 37.6 %collective-permute-start.6 = (bf16[8,2,128,256]{3,2,1,0:T(8,128)(2,1)}, bf16[8,2,128,256]{3,2,1,0:T(8,128)(2,1)}, u32[]{:S(2)}, u32[]{:S(2)}) collective-permute-start(bf16[8,2,128,256]{3,2,1,0:T(8,128)(2,1)} %get-tuple-element.23), channel_id=1, source_target_pairs={{16,0},{17,1},{18,2},{19,3},{20,4},{21,5},{22,6},{23,7},{24,8},{25... | collective-permute-start | bytes 3145736 | tf_op jit(solution)/shard_map/ppermute | solution.py:383
  55.4 30.7 %collective-permute-start.5 = (bf16[8,2,128,256]{3,2,1,0:T(8,128)(2,1)}, bf16[8,2,128,256]{3,2,1,0:T(8,128)(2,1)}, u32[]{:S(2)}, u32[]{:S(2)}) collective-permute-start(bf16[8,2,128,256]{3,2,1,0:T(8,128)(2,1)} %get-tuple-element.24), channel_id=1, source_target_pairs={{0,16},{1,17},{2,18},{3,19},{4,20},{5,21},{6,22},{7,23},{8,24},{9,... | collective-permute-start | bytes 3145736 | tf_op jit(solution)/shard_map/ppermute | solution.py:383
  57.3 21.1 %collective-permute-start.3 = (s32[2]{0:T(128)S(1)}, s32[2]{0:T(128)S(1)}, u32[]{:S(2)}, u32[]{:S(2)}) collective-permute-start(s32[2]{0:T(128)S(1)} %get-tuple-element.27), channel_id=1, source_target_pairs={{16,0},{17,1},{18,2},{19,3},{20,4},{21,5},{22,6},{23,7},{24,8},{25... | collective-permute-start | bytes 32 | tf_op jit(solution)/shard_map/ppermute | solution.py:374
  63.4 21.3 %collective-permute-start.4 = (s32[2]{0:T(128)S(1)}, s32[2]{0:T(128)S(1)}, u32[]{:S(2)}, u32[]{:S(2)}) collective-permute-start(s32[2]{0:T(128)S(1)} %get-tuple-element.28), channel_id=1, source_target_pairs={{0,16},{1,17},{2,18},{3,19},{4,20},{5,21},{6,22},{7,23},{8,24},{9,... | collective-permute-start | bytes 32 | tf_op jit(solution)/shard_map/ppermute | solution.py:374
  84.8 1.3 copy-start.5
  109.8 34.2 %all-to-all-start.3 = ((bf16[16,2,128,128]{3,2,1,0:T(8,128)(2,1)}), bf16[16,2,128,128]{3,2,1,0:T(8,128)(2,1)S(1)}, u32[]{:S(2)}, u32[]{:S(2)}) async-start(bf16[16,2,128,128]{3,2,1,0:T(8,128)(2,1)} %get-tuple-element.20), calls=%async_computation.3 | async-start | bytes 2097152 | tf_op jit(solution)/shard_map/all_to_all | solution.py:386
  116.0 24.1 %collective-permute-start.7 = (bf16[6,2,128,256]{3,2,1,0:T(8,128)(2,1)}, bf16[6,2,128,256]{3,2,1,0:T(8,128)(2,1)S(1)}, u32[]{:S(2)}, u32[]{:S(2)}) collective-permute-start(bf16[6,2,128,256]{3,2,1,0:T(8,128)(2,1)} %get-tuple-element.18), channel_id=1, source_target_pairs={{0,16},{1,17},{2,18},{3,19},{4,20},{5,21},{6,22},{7,23},{8,24},{9,... | collective-permute-start | bytes 2359304 | tf_op jit(solution)/shard_map/ppermute | solution.py:385
  118.0 23.4 %collective-permute-start.8 = (bf16[6,2,128,256]{3,2,1,0:T(8,128)(2,1)}, bf16[6,2,128,256]{3,2,1,0:T(8,128)(2,1)S(1)}, u32[]{:S(2)}, u32[]{:S(2)}) collective-permute-start(bf16[6,2,128,256]{3,2,1,0:T(8,128)(2,1)} %get-tuple-element.19), channel_id=1, source_target_pairs={{16,0},{17,1},{18,2},{19,3},{20,4},{21,5},{22,6},{23,7},{24,8},{25... | collective-permute-start | bytes 2359304 | tf_op jit(solution)/shard_map/ppermute | solution.py:385
  144.0 34.4 %all-to-all-start.2 = ((bf16[16,2,128,256]{3,2,1,0:T(8,128)(2,1)}), bf16[16,2,128,256]{3,2,1,0:T(8,128)(2,1)S(1)}, u32[]{:S(2)}, u32[]{:S(2)}) async-start(bf16[16,2,128,256]{3,2,1,0:T(8,128)(2,1)} %shard_map.49), calls=%async_computation.2 | async-start | bytes 4194304 | tf_op jit(solution)/shard_map/all_to_all | solution.py:387

commit v4 on v3

--- a/solution.py
+++ b/solution.py
@@ -17,8 +17,6 @@
 RING = 4
 GROUP = RING * TILES
 HALO = SPAN * TILES
-NAMED = 2
-BACK = TILES + NAMED
 EXT = GROUP + 2 * HALO
 LOCAL = 2
 SLOTS = WIN + LISTED
@@ -134,41 +132,27 @@
     )(flip, dkv, held)
 
 
-def add_kernel(ask_ref, own_ref, prev_ref, next_ref, out_ref):
-    zero = jnp.zeros((), F32)
+def add_kernel(own_ref, prev_ref, next_ref, out_ref):
     for b in range(GROUP):
         for h in range(LOCAL):
-            total = own_ref[b, h].astype(F32)
-            if b < TILES:
-                total = total + prev_ref[b, h].astype(F32)
-            elif b < 2 * TILES:
-                for i in range(NAMED):
-                    hit = ask_ref[1, i] == b - TILES
-                    total = total + jnp.where(hit, prev_ref[TILES + i, h].astype(F32), zero)
-            elif b < GROUP - TILES:
-                for i in range(NAMED):
-                    hit = ask_ref[0, i] == b - (GROUP - 2 * TILES)
-                    total = total + jnp.where(hit, next_ref[i, h].astype(F32), zero)
-            else:
-                total = total + next_ref[NAMED + b - (GROUP - TILES), h].astype(F32)
-            out_ref[b, h] = total.astype(BF16)
-
-
-def add_halo(ask, own, from_prev, from_next):
+            more = prev_ref[b, h] if b < HALO else next_ref[b - HALO, h]
+            out_ref[b, h] = (own_ref[b, h].astype(F32) + more.astype(F32)).astype(BF16)
+
+
+def add_halo(own, from_prev, from_next):
     return pl.pallas_call(
         add_kernel,
         out_shape=jax.ShapeDtypeStruct((GROUP, LOCAL, BLK, 2 * HD), BF16),
-        in_specs=[SMEM] + [VMEM] * 3,
+        in_specs=[VMEM] * 3,
         out_specs=VMEM,
-        compiler_params=pltpu.CompilerParams(vmem_limit_bytes=12 << 20),
+        compiler_params=pltpu.CompilerParams(vmem_limit_bytes=14 << 20),
         cost_estimate=pl.CostEstimate(flops=4 << 20, bytes_accessed=8 << 20, transcendentals=0),
-    )(ask, own, from_prev, from_next)
+    )(own, from_prev, from_next)
 
 
 def attention_kernel(
     place_ref,
     live_ref,
-    want_ref,
     kv_ref,
     before_ref,
     after_ref,
@@ -199,14 +183,9 @@
         ]
         there = [
             (dqs.at[h], dq_ref.at[:, h]),
-            (outs.at[h, pl.ds(TILES, TILES)], tobefore_ref.at[pl.ds(NAMED, TILES), h]),
-            (outs.at[h, pl.ds(HALO, TILES)], toafter_ref.at[pl.ds(0, TILES), h]),
+            (outs.at[h, pl.ds(0, HALO)], tobefore_ref.at[:, h]),
+            (outs.at[h, pl.ds(HALO, HALO)], toafter_ref.at[:, h]),
         ]
-        for i in range(NAMED):
-            there.append((outs.at[h, want_ref[0, i]], tobefore_ref.at[i, h]))
-            there.append(
-                (outs.at[h, HALO + TILES + want_ref[1, i]], toafter_ref.at[TILES + i, h])
-            )
         loads.append([pltpu.make_async_copy(s, d, came.at[h, i]) for i, (s, d) in enumerate(here)])
         stores.append([pltpu.make_async_copy(s, d, left.at[h, i]) for i, (s, d) in enumerate(there)])
     for h in range(LOCAL):
@@ -286,7 +265,7 @@
                 c.wait()
         lax.fori_loop(0, GROUP // SIDES, step(h), 0)
         outs[h, 0:HALO] = (acc[h, 0:HALO] * factor).astype(BF16)
-        outs[h, HALO:] = (acc[h, HALO + GROUP :] * factor).astype(BF16)
+        outs[h, HALO : 2 * HALO] = (acc[h, HALO + GROUP : EXT] * factor).astype(BF16)
         for c in stores[h]:
             c.start()
         own_ref[:, h] = (acc[h, HALO : HALO + GROUP] * factor).astype(BF16)
@@ -295,16 +274,16 @@
             c.wait()
 
 
-def attention(places, live, wants, kv, before, after, qd):
+def attention(places, live, kv, before, after, qd):
     return pl.pallas_call(
         attention_kernel,
         out_shape=[
             pltpu.HBM((GROUP, LOCAL, BLK, HD), BF16),
             jax.ShapeDtypeStruct((GROUP, LOCAL, BLK, 2 * HD), BF16),
-            pltpu.HBM((BACK, LOCAL, BLK, 2 * HD), BF16),
-            pltpu.HBM((BACK, LOCAL, BLK, 2 * HD), BF16),
+            pltpu.HBM((HALO, LOCAL, BLK, 2 * HD), BF16),
+            pltpu.HBM((HALO, LOCAL, BLK, 2 * HD), BF16),
         ],
-        in_specs=[SMEM, SMEM, SMEM, HBM, HBM, HBM, HBM],
+        in_specs=[SMEM, SMEM, HBM, HBM, HBM, HBM],
         out_specs=[HBM, VMEM, HBM, HBM],
         scratch_shapes=[
             pltpu.VMEM((LOCAL, EXT, BLK, 2 * HD), BF16),
@@ -317,13 +296,17 @@
             pltpu.VMEM((LOCAL, GROUP, BLK, HD), BF16),
             pltpu.VMEM((LOCAL, 2 * HALO, BLK, 2 * HD), BF16),
             pltpu.SemaphoreType.DMA((LOCAL, 4)),
-            pltpu.SemaphoreType.DMA((LOCAL, 3 + 2 * NAMED)),
+            pltpu.SemaphoreType.DMA((LOCAL, 3)),
         ],
         compiler_params=pltpu.CompilerParams(vmem_limit_bytes=30 << 20),
         cost_estimate=pl.CostEstimate(
             flops=4_800_000_000, bytes_accessed=16 << 20, transcendentals=4_000_000
         ),
-    )(places, live, wants, *(pltpu.with_memory_space_constraint(x, pltpu.HBM) for x in (kv, before, after, qd)))
+    )(
+        places,
+        live,
+        *(pltpu.with_memory_space_constraint(x, pltpu.HBM) for x in (kv, before, after, qd)),
+    )
 
 
 def shards(qkv, grad_out, key_lists, live_counts):
@@ -361,30 +344,16 @@
     live = jnp.concatenate([window_ok, listed_ok], axis=1).astype(jnp.int32)
     places = jnp.concatenate([window, named[:, :LISTED]], axis=1) - plane * GROUP + HALO
 
-    order = jnp.arange(TILES, dtype=jnp.int32)
-    ends = jnp.stack([order, order + EXT - TILES])
-    needed = jnp.any(places[None, :, :, None] == ends[:, None, None, :], axis=(1, 2))
-    wants = jnp.stack(
-        [
-            jnp.min(jnp.where(needed, order, TILES - 1), axis=1),
-            jnp.max(jnp.where(needed, order, 0), axis=1),
-        ],
-        axis=1,
-    ).astype(jnp.int32)
-    ask = jnp.stack([to_prev(wants[0]), to_next(wants[1])])
-    once = jnp.where(ask[:, 1] == ask[:, 0], -1, ask[:, 1])
-    ask = jnp.stack([ask[:, 0], once], axis=1)
-
     swap = functools.partial(lax.all_to_all, axis_name=team, split_axis=0, concat_axis=0, tiled=True)
     qd = send_queries(flip, qkv, grad_out)
     kv = swap(send_pairs(flip, qkv))
     kv, qd = lax.optimization_barrier((kv, qd))
-    qd, ask = lax.optimization_barrier((swap(qd), ask))
+    qd = swap(qd)
     before, after = to_next(kv[GROUP - HALO :]), to_prev(kv[:HALO])
-    dq, own, tobefore, toafter = attention(places, live, wants, kv, before, after, qd)
+    dq, own, tobefore, toafter = attention(places, live, kv, before, after, qd)
     from_prev, from_next = to_next(toafter), to_prev(tobefore)
     held = join_early(flip, swap(dq))
-    dkv = swap(add_halo(ask, own, from_prev, from_next))
+    dkv = swap(add_halo(own, from_prev, from_next))
     return join_late(flip, dkv, held)
 
 

time: 182 us -> 177 us (0.973)
  starting transfers between devices: 54.6 us -> 49.1 us
  waiting for transfers between devices: 81.1 us -> 84.2 us
  local copies, waits for them, and re-layouts: 11.5 us -> 8.47 us
    ppermute x2, waiting for transfers between devices: 0.01 us -> 26 us  [shards(): before, after = (to_next(kv[GROUP - HALO:]), to_prev(kv[:HALO]))]
    ppermute x2 -> x0, waiting for transfers between devices: 19 us -> none  [shards(): ask = jnp.stack([to_prev(wants[0]), to_next(wants[1])])]
    ppermute x3, waiting for transfers between devices: 18.1 us -> 0.01 us  [shards(): lax.ppermute(named, 'x', [(i, (i + step) % RING) for i in range(RING)])]
    all_to_all x1, waiting for transfers between devices: 0.01 us -> 16.9 us  [shards(): kv = swap(send_pairs(flip, qkv))]
    ppermute x2 -> x0, starting transfers between devices: 7.95 us -> none  [shards(): ask = jnp.stack([to_prev(wants[0]), to_next(wants[1])])]
    ppermute x2, waiting for transfers between devices: 17.4 us -> 14.8 us  [shards(): from_prev, from_next = (to_next(toafter), to_prev(tobefore))]
    unnamed x16 -> x14, local copies, waits for them, and re-layouts: 7.07 us -> 5.78 us
  transfers between devices with their start and end apart: 13 -> 11, of which waited for: 6 -> 6; matrix products, arithmetic and copies ran while one was open for 3% -> 2% of each run, Pallas kernels for 3% -> 3%
where the time goes in v4:
time: 177 us; the launch traced here: 175 us
  waiting for transfers between devices  84.2 us (48%)
  starting transfers between devices  49.1 us (28%)
  Pallas kernels  32 us (18%)
  local copies, waits for them, and re-layouts  8.47 us (5%)
    all_to_all x1, waiting for transfers between devices, shards(): dkv = swap(add_halo(own, from_prev, from_next))  26.5 us
    ppermute x2, waiting for transfers between devices, shards(): before, after = (to_next(kv[GROUP - HALO:]), to_prev(kv[:HALO]))  26 us
    pallas_call x1, Pallas kernels, attention(): pl.pallas_call(attention_kernel, out_shape=[pltpu.HBM((GROUP, LOCAL, BLK,...  23.7 us
    all_to_all x1, waiting for transfers between devices, shards(): kv = swap(send_pairs(flip, qkv))  16.9 us
    ppermute x2, waiting for transfers between devices, shards(): from_prev, from_next = (to_next(toafter), to_prev(tobefore))  14.8 us
    ppermute x2, starting transfers between devices, shards(): before, after = (to_next(kv[GROUP - HALO:]), to_prev(kv[:HALO]))  10.4 us
    ppermute x2, starting transfers between devices, shards(): from_prev, from_next = (to_next(toafter), to_prev(tobefore))  7.95 us
    all_to_all x1, starting transfers between devices, shards(): held = join_early(flip, swap(dq))  7 us
  transfers between devices with their start and end apart: 11, of which 6 were waited for; matrix products, arithmetic and copies ran while one was open for 2% of the time, Pallas kernels for 3%

profile of v4, /device:TPU:16, one launch (start us, length us, event | category | flops | bytes accessed | tf_op | source)
XLA Modules:
  0.0 174.6 jit_solution(7097882545851481366)
XLA Ops:
  0.0 1.9 %copy-done = bf16[128,12288]{1,0:T(8,128)(2,1)S(1)} copy-done((bf16[128,12288]{1,0:T(8,128)(2,1)S(1)}, bf16[128,12288]{1,0:T(8,128)(2,1)}, u32[]{:S(2)}) %copy-start) | copy-done | bytes 3145752
  1.9 0.7 shard_map.46
  2.7 1.3 copy-done.3
  4.0 5.4 %all-to-all-start = ((bf16[16,2,128,256]{3,2,1,0:T(8,128)(2,1)}), bf16[16,2,128,256]{3,2,1,0:T(8,128)(2,1)}, u32[]{:S(2)}, u32[]{:S(2)}) async-start(bf16[16,2,128,256]{3,2,1,0:T(8,128)(2,1)} %copy-done.3), calls=%async_computation | async-start | bytes 4194304 | tf_op jit(solution)/shard_map/all_to_all | solution.py:349
  9.4 0.1 copy.9
  9.6 3.4 %collective-permute-start.1 = (s32[4,5]{1,0:T(4,128)S(1)}, s32[4,5]{1,0:T(4,128)S(1)}, u32[]{:S(2)}, u32[]{:S(2)}) collective-permute-start(s32[4,5]{1,0:T(4,128)S(1)} %pad_add_fusion.1), channel_id=1, source_target_pairs={{0,8},{4,12},{8,0},{12,4},{1,9},{5,13},{9,1},{13,5},{2,10},{6,14},... | collective-permute-start | bytes 248 | tf_op jit(solution)/shard_map/ppermute | solution.py:337
  13.0 0.6 collective-permute-start
  13.6 2.7 %collective-permute-start.2 = (s32[4,5]{1,0:T(4,128)S(1)}, s32[4,5]{1,0:T(4,128)S(1)}, u32[]{:S(2)}, u32[]{:S(2)}) collective-permute-start(s32[4,5]{1,0:T(4,128)S(1)} %pad_add_fusion.1), channel_id=1, source_target_pairs={{0,12},{4,0},{8,4},{12,8},{1,13},{5,1},{9,5},{13,9},{2,14},{6,2},{... | collective-permute-start | bytes 248 | tf_op jit(solution)/shard_map/ppermute | solution.py:337
  16.2 1.2 copy-done.4
  17.5 1.5 shard_map.47
  19.0 1.3 copy-done.2
  20.4 16.9 %all-to-all-done.kv_ref = bf16[16,2,128,256]{3,2,1,0:T(8,128)(2,1)} async-done(((bf16[16,2,128,256]{3,2,1,0:T(8,128)(2,1)}), bf16[16,2,128,256]{3,2,1,0:T(8,128)(2,1)}, u32[]{:S(2)}, u32[]{:S(2)}) %all-to-all-start) | async-done | bytes 2097184 | tf_op jit(solution)/shard_map/all_to_all | solution.py:349
  37.2 4.9 %all-to-all-start.1 = ((bf16[16,2,128,256]{3,2,1,0:T(8,128)(2,1)}), bf16[16,2,128,256]{3,2,1,0:T(8,128)(2,1)}, u32[]{:S(2)}, u32[]{:S(2)}) async-start(bf16[16,2,128,256]{3,2,1,0:T(8,128)(2,1)} %copy-done.2), calls=%async_computation.1 | async-start | bytes 4194304 | tf_op jit(solution)/shard_map/all_to_all | solution.py:351
  42.3 1.7 fusion.4
  44.0 8.5 %collective-permute-start.4 = (bf16[8,2,128,256]{3,2,1,0:T(8,128)(2,1)S(1)}, bf16[8,2,128,256]{3,2,1,0:T(8,128)(2,1)}, u32[]{:S(2)}, u32[]{:S(2)}) collective-permute-start(bf16[8,2,128,256]{3,2,1,0:T(8,128)(2,1)S(1)} %get-tuple-element.17), channel_id=1, source_target_pairs={{16,0},{17,1},{18,2},{19,3},{20,4},{21,5},{22,6},{23,7},{24,8},{25... | collective-permute-start | bytes 3145736 | tf_op jit(solution)/shard_map/ppermute | solution.py:352
  52.4 1.9 %collective-permute-start.3 = (bf16[8,2,128,256]{3,2,1,0:T(8,128)(2,1)S(1)}, bf16[8,2,128,256]{3,2,1,0:T(8,128)(2,1)}, u32[]{:S(2)}, u32[]{:S(2)}) collective-permute-start(bf16[8,2,128,256]{3,2,1,0:T(8,128)(2,1)S(1)} %get-tuple-element.18), channel_id=1, source_target_pairs={{0,16},{1,17},{2,18},{3,19},{4,20},{5,21},{6,22},{7,23},{8,24},{9,... | collective-permute-start | bytes 3145736 | tf_op jit(solution)/shard_map/ppermute | solution.py:352
  54.5 0.1 broadcast_in_dim.21
  54.6 0.6 gather_fusion
  55.3 0.2 slice_reduce_fusion
  55.7 19.7 %collective-permute-done.4.after_ref = bf16[8,2,128,256]{3,2,1,0:T(8,128)(2,1)} collective-permute-done((bf16[8,2,128,256]{3,2,1,0:T(8,128)(2,1)S(1)}, bf16[8,2,128,256]{3,2,1,0:T(8,128)(2,1)}, u32[]{:S(2)}, u32[]{:S(2)}) %collective-permute-start.4) | collective-permute-done | bytes 1048608 | tf_op jit(solution)/shard_map/ppermute | solution.py:352
  75.3 6.3 %collective-permute-done.3.before_ref = bf16[8,2,128,256]{3,2,1,0:T(8,128)(2,1)} collective-permute-done((bf16[8,2,128,256]{3,2,1,0:T(8,128)(2,1)S(1)}, bf16[8,2,128,256]{3,2,1,0:T(8,128)(2,1)}, u32[]{:S(2)}, u32[]{:S(2)}) %collective-permute-start.3) | collective-permute-done | bytes 1048608 | tf_op jit(solution)/shard_map/ppermute | solution.py:352
  81.7 23.7 %shard_map.48 = (bf16[16,2,128,128]{3,2,1,0:T(8,128)(2,1)}, bf16[16,2,128,256]{3,2,1,0:T(8,128)(2,1)S(1)}, bf16[8,2,128,256]{3,2,1,0:T(8,128)(2,1)}, bf16[8,2,128,256]{3,2,1,0:T(8,128)(2,1)}) custom-call(s32[16,7]{1,0:T(8,128)S(1)} %fusion.place_ref, s32[16,7]{1,0:T(8,128)S(1)} %add_convert_fusion.live_ref, bf16[16,2,128,256]{3,2,1,0:T(8,128)(2,1)} %all-to-all-done.kv_ref, ...), custom_call_target="tpu_custom_call" | custom-call | flops 4800000000 | bytes 16777216 | tf_op jit(solution)/shard_map/pallas_call | solution.py:278
  105.3 1.9 %collective-permute-start.5 = (bf16[8,2,128,256]{3,2,1,0:T(8,128)(2,1)}, bf16[8,2,128,256]{3,2,1,0:T(8,128)(2,1)}, u32[]{:S(2)}, u32[]{:S(2)}) collective-permute-start(bf16[8,2,128,256]{3,2,1,0:T(8,128)(2,1)} %get-tuple-element.14), channel_id=1, source_target_pairs={{0,16},{1,17},{2,18},{3,19},{4,20},{5,21},{6,22},{7,23},{8,24},{9,... | collective-permute-start | bytes 3145736 | tf_op jit(solution)/shard_map/ppermute | solution.py:354
  107.3 6.0 %collective-permute-start.6 = (bf16[8,2,128,256]{3,2,1,0:T(8,128)(2,1)}, bf16[8,2,128,256]{3,2,1,0:T(8,128)(2,1)}, u32[]{:S(2)}, u32[]{:S(2)}) collective-permute-start(bf16[8,2,128,256]{3,2,1,0:T(8,128)(2,1)} %get-tuple-element.15), channel_id=1, source_target_pairs={{16,0},{17,1},{18,2},{19,3},{20,4},{21,5},{22,6},{23,7},{24,8},{25... | collective-permute-start | bytes 3145736 | tf_op jit(solution)/shard_map/ppermute | solution.py:354
  113.3 7.0 %all-to-all-start.3 = ((bf16[16,2,128,128]{3,2,1,0:T(8,128)(2,1)}), bf16[16,2,128,128]{3,2,1,0:T(8,128)(2,1)S(1)}, u32[]{:S(2)}, u32[]{:S(2)}) async-start(bf16[16,2,128,128]{3,2,1,0:T(8,128)(2,1)} %get-tuple-element.16), calls=%async_computation.3 | async-start | bytes 2097152 | tf_op jit(solution)/shard_map/all_to_all | solution.py:355
  120.3 13.6 %collective-permute-done.5.prev_ref = bf16[8,2,128,256]{3,2,1,0:T(8,128)(2,1)} collective-permute-done((bf16[8,2,128,256]{3,2,1,0:T(8,128)(2,1)}, bf16[8,2,128,256]{3,2,1,0:T(8,128)(2,1)}, u32[]{:S(2)}, u32[]{:S(2)}) %collective-permute-start.5) | collective-permute-done | bytes 1048608 | tf_op jit(solution)/shard_map/ppermute | solution.py:354
  133.9 1.2 collective-permute-done.6.next_ref
  135.1 3.3 %shard_map.49 = bf16[16,2,128,256]{3,2,1,0:T(8,128)(2,1)} custom-call(bf16[16,2,128,256]{3,2,1,0:T(8,128)(2,1)S(1)} %get-tuple-element.13.own_ref, bf16[8,2,128,256]{3,2,1,0:T(8,128)(2,1)} %collective-permute-done.5.prev_ref, bf16[8,2,128,256]{3,2,1,0:T(8,128)(2,1)} %collective-permute-done.6.next_ref), custom_call_target="tpu_custom_call" | custom-call | flops 4194304 | bytes 8388608 | tf_op jit(solution)/shard_map/pallas_call | solution.py:143
  138.5 6.8 %all-to-all-start.2 = ((bf16[16,2,128,256]{3,2,1,0:T(8,128)(2,1)}), bf16[16,2,128,256]{3,2,1,0:T(8,128)(2,1)S(1)}, u32[]{:S(2)}, u32[]{:S(2)}) async-start(bf16[16,2,128,256]{3,2,1,0:T(8,128)(2,1)} %shard_map.49), calls=%async_computation.2 | async-start | bytes 4194304 | tf_op jit(solution)/shard_map/all_to_all | solution.py:356
  145.3 1.2 shard_map.50.held_ref
  146.5 26.5 %all-to-all-done.2.dkv_ref = bf16[16,2,128,256]{3,2,1,0:T(8,128)(2,1)S(1)} async-done(((bf16[16,2,128,256]{3,2,1,0:T(8,128)(2,1)}), bf16[16,2,128,256]{3,2,1,0:T(8,128)(2,1)S(1)}, u32[]{:S(2)}, u32[]{:S(2)}) %all-to-all-start.2) | async-done | bytes 2097184 | tf_op jit(solution)/shard_map/all_to_all | solution.py:356
  173.0 1.6 shard_map.51
  (29 shorter events, 0.8 us)
Async XLA Ops:
  0.0 1.9 %copy-start = (bf16[128,12288]{1,0:T(8,128)(2,1)S(1)}, bf16[128,12288]{1,0:T(8,128)(2,1)}, u32[]{:S(2)}) copy-start(bf16[128,12288]{1,0:T(8,128)(2,1)} %qkv_ref.3) | copy-start | bytes 9437188
  2.6 1.3 copy-start.3
  4.0 5.5 %copy-start.6 = (s32[4]{0:T(128)S(1)}, s32[4]{0:T(128)}, u32[]{:S(2)}) copy-start(s32[4]{0:T(128)} %param.7) | copy-start | bytes 52
  4.0 5.6 %copy-start.5 = (s32[4,4]{1,0:T(4,128)S(1)}, s32[4,4]{1,0:T(4,128)}, u32[]{:S(2)}) copy-start(s32[4,4]{1,0:T(4,128)} %param.6) | copy-start | bytes 196
  4.0 12.3 %copy-start.1 = (bf16[128,12288]{1,0:T(8,128)(2,1)S(1)}, bf16[128,12288]{1,0:T(8,128)(2,1)}, u32[]{:S(2)}) copy-start(bf16[128,12288]{1,0:T(8,128)(2,1)} %qkv_ref.3) | copy-start | bytes 9437188
  4.0 33.3 %all-to-all-start = ((bf16[16,2,128,256]{3,2,1,0:T(8,128)(2,1)}), bf16[16,2,128,256]{3,2,1,0:T(8,128)(2,1)}, u32[]{:S(2)}, u32[]{:S(2)}) async-start(bf16[16,2,128,256]{3,2,1,0:T(8,128)(2,1)} %copy-done.3), calls=%async_computation | async-start | bytes 4194304 | tf_op jit(solution)/shard_map/all_to_all | solution.py:349
  9.6 45.0 %collective-permute-start.1 = (s32[4,5]{1,0:T(4,128)S(1)}, s32[4,5]{1,0:T(4,128)S(1)}, u32[]{:S(2)}, u32[]{:S(2)}) collective-permute-start(s32[4,5]{1,0:T(4,128)S(1)} %pad_add_fusion.1), channel_id=1, source_target_pairs={{0,8},{4,12},{8,0},{12,4},{1,9},{5,13},{9,1},{13,5},{2,10},{6,14},... | collective-permute-start | bytes 248 | tf_op jit(solution)/shard_map/ppermute | solution.py:337
  13.0 41.6 %collective-permute-start = (s32[4,5]{1,0:T(4,128)S(1)}, s32[4,5]{1,0:T(4,128)S(1)}, u32[]{:S(2)}, u32[]{:S(2)}) collective-permute-start(s32[4,5]{1,0:T(4,128)S(1)} %pad_add_fusion.1), channel_id=1, source_target_pairs={{0,4},{4,8},{8,12},{12,0},{1,5},{5,9},{9,13},{13,1},{2,6},{6,10},{... | collective-permute-start | bytes 248 | tf_op jit(solution)/shard_map/ppermute | solution.py:337
  13.6 41.0 %collective-permute-start.2 = (s32[4,5]{1,0:T(4,128)S(1)}, s32[4,5]{1,0:T(4,128)S(1)}, u32[]{:S(2)}, u32[]{:S(2)}) collective-permute-start(s32[4,5]{1,0:T(4,128)S(1)} %pad_add_fusion.1), channel_id=1, source_target_pairs={{0,12},{4,0},{8,4},{12,8},{1,13},{5,1},{9,5},{13,9},{2,14},{6,2},{... | collective-permute-start | bytes 248 | tf_op jit(solution)/shard_map/ppermute | solution.py:337
  16.2 1.2 copy-start.4
  18.9 1.3 copy-start.2
  37.2 44.4 %all-to-all-start.1 = ((bf16[16,2,128,256]{3,2,1,0:T(8,128)(2,1)}), bf16[16,2,128,256]{3,2,1,0:T(8,128)(2,1)}, u32[]{:S(2)}, u32[]{:S(2)}) async-start(bf16[16,2,128,256]{3,2,1,0:T(8,128)(2,1)} %copy-done.2), calls=%async_computation.1 | async-start | bytes 4194304 | tf_op jit(solution)/shard_map/all_to_all | solution.py:351
  44.0 31.3 %collective-permute-start.4 = (bf16[8,2,128,256]{3,2,1,0:T(8,128)(2,1)S(1)}, bf16[8,2,128,256]{3,2,1,0:T(8,128)(2,1)}, u32[]{:S(2)}, u32[]{:S(2)}) collective-permute-start(bf16[8,2,128,256]{3,2,1,0:T(8,128)(2,1)S(1)} %get-tuple-element.17), channel_id=1, source_target_pairs={{16,0},{17,1},{18,2},{19,3},{20,4},{21,5},{22,6},{23,7},{24,8},{25... | collective-permute-start | bytes 3145736 | tf_op jit(solution)/shard_map/ppermute | solution.py:352
  52.4 29.2 %collective-permute-start.3 = (bf16[8,2,128,256]{3,2,1,0:T(8,128)(2,1)S(1)}, bf16[8,2,128,256]{3,2,1,0:T(8,128)(2,1)}, u32[]{:S(2)}, u32[]{:S(2)}) collective-permute-start(bf16[8,2,128,256]{3,2,1,0:T(8,128)(2,1)S(1)} %get-tuple-element.18), channel_id=1, source_target_pairs={{0,16},{1,17},{2,18},{3,19},{4,20},{5,21},{6,22},{7,23},{8,24},{9,... | collective-permute-start | bytes 3145736 | tf_op jit(solution)/shard_map/ppermute | solution.py:352
  105.3 28.6 %collective-permute-start.5 = (bf16[8,2,128,256]{3,2,1,0:T(8,128)(2,1)}, bf16[8,2,128,256]{3,2,1,0:T(8,128)(2,1)}, u32[]{:S(2)}, u32[]{:S(2)}) collective-permute-start(bf16[8,2,128,256]{3,2,1,0:T(8,128)(2,1)} %get-tuple-element.14), channel_id=1, source_target_pairs={{0,16},{1,17},{2,18},{3,19},{4,20},{5,21},{6,22},{7,23},{8,24},{9,... | collective-permute-start | bytes 3145736 | tf_op jit(solution)/shard_map/ppermute | solution.py:354
  107.3 27.8 %collective-permute-start.6 = (bf16[8,2,128,256]{3,2,1,0:T(8,128)(2,1)}, bf16[8,2,128,256]{3,2,1,0:T(8,128)(2,1)}, u32[]{:S(2)}, u32[]{:S(2)}) collective-permute-start(bf16[8,2,128,256]{3,2,1,0:T(8,128)(2,1)} %get-tuple-element.15), channel_id=1, source_target_pairs={{16,0},{17,1},{18,2},{19,3},{20,4},{21,5},{22,6},{23,7},{24,8},{25... | collective-permute-start | bytes 3145736 | tf_op jit(solution)/shard_map/ppermute | solution.py:354
  113.3 25.2 %all-to-all-start.3 = ((bf16[16,2,128,128]{3,2,1,0:T(8,128)(2,1)}), bf16[16,2,128,128]{3,2,1,0:T(8,128)(2,1)S(1)}, u32[]{:S(2)}, u32[]{:S(2)}) async-start(bf16[16,2,128,128]{3,2,1,0:T(8,128)(2,1)} %get-tuple-element.16), calls=%async_computation.3 | async-start | bytes 2097152 | tf_op jit(solution)/shard_map/all_to_all | solution.py:355
  138.5 34.5 %all-to-all-start.2 = ((bf16[16,2,128,256]{3,2,1,0:T(8,128)(2,1)}), bf16[16,2,128,256]{3,2,1,0:T(8,128)(2,1)S(1)}, u32[]{:S(2)}, u32[]{:S(2)}) async-start(bf16[16,2,128,256]{3,2,1,0:T(8,128)(2,1)} %shard_map.49), calls=%async_computation.2 | async-start | bytes 4194304 | tf_op jit(solution)/shard_map/all_to_all | solution.py:356
